TPU v7x, 128 devices: a whole 4x4x4 slice. The times are simulated.
128 devices in a mesh: ctx: 32 (over y, z, core), tp: 4 (over x).
Axes of the slice: x: 4, y: 4, z: 4, core: 2. Of those that a mesh axis runs over, the one named last changes fastest.
Arguments:
- tokens: bfloat16 [2, 2, 32, 64, 1024], P(None, None, 'ctx'), may hold values from -6 to 6
- norm_gain: float32 [1024], replicated, may hold values from 0.5 to 1.5
- query_weight: bfloat16 [1024, 1024], P(None, 'tp'), may hold values from -0.1875 to 0.1875
- key_weight: bfloat16 [1024, 512], P(None, 'tp'), may hold values from -0.1875 to 0.1875
- value_weight: bfloat16 [1024, 512], P(None, 'tp'), may hold values from -0.1875 to 0.1875
- query_gain: float32 [64], replicated, may hold values from 0.1 to 1.9
- key_gain: float32 [64], replicated, may hold values from 0.1 to 1.9
- out_weight: bfloat16 [1024, 1024], P('tp'), may hold values from -1.5 to 1.5
- post_gain: float32 [1024], replicated, may hold values from 0.5 to 1.5
- gate_weight: bfloat16 [1024, 4608], P(None, 'tp'), may hold values from -0.1875 to 0.1875
- up_weight: bfloat16 [1024, 4608], P(None, 'tp'), may hold values from -0.1875 to 0.1875
- down_weight: bfloat16 [4608, 1024], P('tp'), may hold values from -0.09375 to 0.09375
- cotangent: bfloat16 [2, 2, 32, 64, 1024], P(None, None, 'ctx'), may hold values from -6 to 6
Outputs:
- mixed: bfloat16 [2, 2, 32, 64, 1024], P(None, None, 'ctx')
- input_grad: bfloat16 [2, 2, 32, 64, 1024], P(None, None, 'ctx')
- norm_gain_grad: float32 [1024], replicated
- query_weight_grad: float32 [1024, 1024], P('ctx', 'tp')
- key_weight_grad: float32 [1024, 512], P('ctx', 'tp')
- value_weight_grad: float32 [1024, 512], P('ctx', 'tp')
- query_gain_grad: float32 [64], replicated
- key_gain_grad: float32 [64], replicated
- out_weight_grad: float32 [1024, 1024], P('tp', 'ctx')
- post_gain_grad: float32 [1024], replicated
- gate_weight_grad: float32 [1024, 4608], P('ctx', 'tp')
- up_weight_grad: float32 [1024, 4608], P('ctx', 'tp')
- down_weight_grad: float32 [4608, 1024], P('tp', 'ctx')
All inputs are finite; a program needn't handle non-finite values.
Results may differ from a plain program's by a relative error of at most 0.025.
Values may be sent and summed in bfloat16 or wider, within the bound.
A program may use at most 128 MiB of HBM per device.

v0:
```python
import jax
import jax.numpy as jnp
from jax import lax
from jax.sharding import PartitionSpec as P

HD = 64


EPSILON = 1e-05
ROPE_BASE = 1000000.0


def rope_tables(positions, width):
    exponent = jnp.arange(0, width, 2).astype(jnp.float32) / width
    frequency = jnp.power(ROPE_BASE, -exponent)
    angles = positions.astype(jnp.float32)[:, None] * frequency[None, :]
    return (jnp.cos(angles), jnp.sin(angles))


def rotate(values, cosine, sine_part):
    middle = values.shape[-1] // 2
    leading = values[..., :middle]
    trailing = values[..., middle:]
    cos_rows = cosine[:, None, :]
    sin_rows = sine_part[:, None, :]
    return jnp.concatenate(
        [leading * cos_rows - trailing * sin_rows, trailing * cos_rows + leading * sin_rows], -1
    )


def rotate_back(grads, cosine, sine_part):
    middle = grads.shape[-1] // 2
    leading = grads[..., :middle]
    trailing = grads[..., middle:]
    cos_rows = cosine[:, None, :]
    sin_rows = sine_part[:, None, :]
    return jnp.concatenate(
        [leading * cos_rows + trailing * sin_rows, trailing * cos_rows - leading * sin_rows], -1
    )


def norm_apply(values, gain):
    inverse = lax.rsqrt(jnp.mean(values * values, -1, keepdims=True) + EPSILON)
    return (values * inverse * gain, inverse)


def norm_back(values, inverse, gain, grads):
    scaled = grads * gain
    back = inverse * (
        scaled - values * inverse * inverse * jnp.mean(scaled * values, -1, keepdims=True)
    )
    return (back, grads * values * inverse)


def on_device(
    tokens,
    norm_gain,
    query_weight,
    key_weight,
    value_weight,
    query_gain,
    key_gain,
    out_weight,
    post_gain,
    gate_weight,
    up_weight,
    down_weight,
    cotangent,
):
    seq_count = tokens.shape[0]
    block_len = tokens.shape[3]
    width = tokens.shape[4]
    local_rows = seq_count * 2 * block_len
    ctx_count = lax.axis_size("ctx")
    ctx_place = lax.axis_index("ctx")
    head_count = query_weight.shape[1] // HD
    kv_count = key_weight.shape[1] // HD
    group_size = head_count // kv_count
    score_scale = HD ** (-0.5)
    seq_length = 2 * block_len * ctx_count
    offsets = jnp.arange(block_len, dtype=jnp.int32)
    seq_places = jnp.concatenate(
        [ctx_place * block_len + offsets, (2 * ctx_count - 1 - ctx_place) * block_len + offsets]
    )
    query_places = jnp.tile(seq_places, seq_count)
    all_blocks = jnp.arange(ctx_count, dtype=jnp.int32)
    key_places = jnp.concatenate(
        [
            (all_blocks[:, None] * block_len + offsets[None, :]).reshape(-1),
            ((2 * ctx_count - 1 - all_blocks)[:, None] * block_len + offsets[None, :]).reshape(-1),
        ]
    )
    cosine, sine_part = rope_tables(query_places, HD)
    inputs = tokens.reshape(local_rows, width).astype(jnp.float32)
    normed, inverse_in = norm_apply(inputs, norm_gain)
    normed_low = normed.astype(jnp.bfloat16)
    query_proj = jnp.dot(normed_low, query_weight, preferred_element_type=jnp.float32).reshape(
        local_rows, head_count, HD
    )
    key_proj = jnp.dot(normed_low, key_weight, preferred_element_type=jnp.float32).reshape(
        local_rows, kv_count, HD
    )
    value_low = jnp.dot(normed_low, value_weight, preferred_element_type=jnp.float32).astype(
        jnp.bfloat16
    )
    query_normed, query_inverse = norm_apply(query_proj, query_gain)
    query_low = rotate(query_normed, cosine, sine_part).astype(jnp.bfloat16)
    key_normed, key_inverse = norm_apply(key_proj, key_gain)
    key_low = (
        rotate(key_normed, cosine, sine_part)
        .astype(jnp.bfloat16)
        .reshape(local_rows, kv_count * HD)
    )
    key_shard = key_low.reshape(seq_count, 2, 1, block_len, kv_count * HD)
    value_shard = value_low.reshape(seq_count, 2, 1, block_len, kv_count * HD)
    key_all, value_all = (
        lax.all_gather(key_shard, "ctx", axis=2, tiled=True),
        lax.all_gather(value_shard, "ctx", axis=2, tiled=True),
    )
    key_all = key_all.reshape(seq_count, seq_length, kv_count, HD)
    value_all = value_all.reshape(seq_count, seq_length, kv_count, HD)

    def query_block(seq_index, half_index):
        first = (seq_index * 2 + half_index) * block_len
        rows = query_low[first : first + block_len]
        return rows.reshape(block_len, kv_count, group_size, HD)

    def scores_for(seq_index, half_index, key_side):
        scores = (
            jnp.einsum(
                "qkgd,skd->kgqs",
                query_block(seq_index, half_index),
                key_side,
                preferred_element_type=jnp.float32,
            )
            * score_scale
        )
        places = seq_places[half_index * block_len : (half_index + 1) * block_len]
        visible = key_places[None, :] <= places[:, None]
        return jnp.where(visible, scores, -1e30)

    attended_rows = []
    log_totals = []
    for seq_index in range(seq_count):
        for half_index in range(2):
            scores = scores_for(seq_index, half_index, key_all[seq_index])
            row_max = jnp.max(scores, -1, keepdims=True)
            unnormed = jnp.exp(scores - row_max)
            row_total = jnp.sum(unnormed, -1, keepdims=True)
            probability = (unnormed / row_total).astype(jnp.bfloat16)
            log_totals.append(row_max + jnp.log(row_total))
            mixed_rows = jnp.einsum(
                "kgqs,skd->qkgd",
                probability,
                value_all[seq_index],
                preferred_element_type=jnp.float32,
            )
            attended_rows.append(mixed_rows.reshape(block_len, head_count * HD))
    attended_low = jnp.concatenate(attended_rows, 0).astype(jnp.bfloat16)
    branch_part = jnp.dot(attended_low, out_weight, preferred_element_type=jnp.float32)
    middle = inputs + lax.psum(branch_part.astype(jnp.bfloat16), "tp").astype(jnp.float32)
    post_normed, post_inverse = norm_apply(middle, post_gain)
    post_low = post_normed.astype(jnp.bfloat16)
    gate_proj = jnp.dot(post_low, gate_weight, preferred_element_type=jnp.float32)
    up_proj = jnp.dot(post_low, up_weight, preferred_element_type=jnp.float32)
    gate_sigmoid = jax.nn.sigmoid(gate_proj)
    silu_gate = gate_proj * gate_sigmoid
    hidden_low = (silu_gate * up_proj).astype(jnp.bfloat16)
    mlp_part = jnp.dot(hidden_low, down_weight, preferred_element_type=jnp.float32)
    output = middle + lax.psum(mlp_part.astype(jnp.bfloat16), "tp").astype(jnp.float32)
    out_grad = cotangent.reshape(local_rows, width)
    down_weight_grad = jnp.dot(hidden_low.T, out_grad, preferred_element_type=jnp.float32)
    hidden_grad = jnp.dot(out_grad, down_weight.T, preferred_element_type=jnp.float32)
    gate_grad = (
        hidden_grad * up_proj * gate_sigmoid * (1.0 + gate_proj * (1.0 - gate_sigmoid))
    ).astype(jnp.bfloat16)
    up_grad_rows = (hidden_grad * silu_gate).astype(jnp.bfloat16)
    gate_weight_grad = jnp.dot(post_low.T, gate_grad, preferred_element_type=jnp.float32)
    up_weight_grad = jnp.dot(post_low.T, up_grad_rows, preferred_element_type=jnp.float32)
    post_part = jnp.dot(gate_grad, gate_weight.T, preferred_element_type=jnp.float32) + jnp.dot(
        up_grad_rows, up_weight.T, preferred_element_type=jnp.float32
    )
    post_grad = lax.psum(post_part.astype(jnp.bfloat16), "tp").astype(jnp.float32)
    back_middle, post_gain_term = norm_back(middle, post_inverse, post_gain, post_grad)
    middle_grad = out_grad.astype(jnp.float32) + back_middle
    middle_low = middle_grad.astype(jnp.bfloat16)
    out_weight_grad = jnp.dot(attended_low.T, middle_low, preferred_element_type=jnp.float32)
    attended_grad = jnp.dot(middle_low, out_weight.T, preferred_element_type=jnp.float32).astype(
        jnp.bfloat16
    )
    key_back, value_back = (
        lax.all_gather(key_shard, "ctx", axis=2, tiled=True),
        lax.all_gather(value_shard, "ctx", axis=2, tiled=True),
    )
    key_back = key_back.reshape(seq_count, seq_length, kv_count, HD)
    value_back = value_back.reshape(seq_count, seq_length, kv_count, HD)
    key_grad_list = []
    value_grad_list = []
    query_grads = []
    for seq_index in range(seq_count):
        key_grad_sum = jnp.zeros((seq_length, kv_count, HD), jnp.float32)
        value_grad_sum = jnp.zeros((seq_length, kv_count, HD), jnp.float32)
        for half_index in range(2):
            block_number = seq_index * 2 + half_index
            scores = scores_for(seq_index, half_index, key_back[seq_index])
            probability = jnp.exp(scores - log_totals[block_number])
            grad_block = attended_grad[
                block_number * block_len : (block_number + 1) * block_len
            ].reshape(block_len, kv_count, group_size, HD)
            prob_grad = jnp.einsum(
                "qkgd,skd->kgqs",
                grad_block,
                value_back[seq_index],
                preferred_element_type=jnp.float32,
            )
            delta_rows = jnp.sum(probability * prob_grad, -1, keepdims=True)
            score_grad = (probability * (prob_grad - delta_rows)).astype(jnp.bfloat16)
            q_grad_rows = jnp.einsum(
                "kgqs,skd->qkgd",
                score_grad,
                key_back[seq_index],
                preferred_element_type=jnp.float32,
            )
            query_grads.append(q_grad_rows.reshape(block_len, head_count, HD) * score_scale)
            key_grad_sum = (
                key_grad_sum
                + jnp.einsum(
                    "kgqs,qkgd->skd",
                    score_grad,
                    query_block(seq_index, half_index),
                    preferred_element_type=jnp.float32,
                )
                * score_scale
            )
            value_grad_sum = value_grad_sum + jnp.einsum(
                "kgqs,qkgd->skd",
                probability.astype(jnp.bfloat16),
                grad_block,
                preferred_element_type=jnp.float32,
            )
        key_grad_list.append(key_grad_sum)
        value_grad_list.append(value_grad_sum)
    key_own, value_own = (
        lax.psum_scatter(
            jnp.stack(key_grad_list, 0)
            .reshape(seq_count, 2, ctx_count, block_len, kv_count * HD)
            .astype(jnp.bfloat16),
            "ctx",
            scatter_dimension=2,
            tiled=True,
        ).astype(jnp.float32),
        lax.psum_scatter(
            jnp.stack(value_grad_list, 0)
            .reshape(seq_count, 2, ctx_count, block_len, kv_count * HD)
            .astype(jnp.bfloat16),
            "ctx",
            scatter_dimension=2,
            tiled=True,
        ).astype(jnp.float32),
    )
    key_own = key_own.reshape(local_rows, kv_count, HD)
    value_grad_low = value_own.reshape(local_rows, kv_count * HD).astype(jnp.bfloat16)
    query_rot_grad = rotate_back(jnp.concatenate(query_grads, 0), cosine, sine_part)
    query_back, query_gain_term = norm_back(query_proj, query_inverse, query_gain, query_rot_grad)
    query_grad_low = query_back.reshape(local_rows, head_count * HD).astype(jnp.bfloat16)
    key_rot_grad = rotate_back(key_own, cosine, sine_part)
    key_back_rows, key_gain_term = norm_back(key_proj, key_inverse, key_gain, key_rot_grad)
    key_grad_low = key_back_rows.reshape(local_rows, kv_count * HD).astype(jnp.bfloat16)
    query_weight_grad = jnp.dot(normed_low.T, query_grad_low, preferred_element_type=jnp.float32)
    key_weight_grad = jnp.dot(normed_low.T, key_grad_low, preferred_element_type=jnp.float32)
    value_weight_grad = jnp.dot(normed_low.T, value_grad_low, preferred_element_type=jnp.float32)
    input_part = (
        jnp.dot(query_grad_low, query_weight.T, preferred_element_type=jnp.float32)
        + jnp.dot(key_grad_low, key_weight.T, preferred_element_type=jnp.float32)
        + jnp.dot(value_grad_low, value_weight.T, preferred_element_type=jnp.float32)
    )
    normed_grad, query_gain_sum, key_gain_sum = (
        lax.psum(input_part.astype(jnp.bfloat16), "tp").astype(jnp.float32),
        lax.psum(jnp.sum(query_gain_term, (0, 1)).astype(jnp.bfloat16), "tp").astype(jnp.float32),
        lax.psum(jnp.sum(key_gain_term, (0, 1)).astype(jnp.bfloat16), "tp").astype(jnp.float32),
    )
    back_inputs, norm_gain_term = norm_back(inputs, inverse_in, norm_gain, normed_grad)
    input_grad = (
        (middle_grad + back_inputs).astype(jnp.bfloat16).reshape(seq_count, 2, 1, block_len, width)
    )
    norm_gain_grad, post_gain_grad, query_gain_grad, key_gain_grad = lax.psum(
        (jnp.sum(norm_gain_term, 0), jnp.sum(post_gain_term, 0), query_gain_sum, key_gain_sum),
        "ctx",
    )
    query_weight_grad, key_weight_grad, value_weight_grad, gate_weight_grad, up_weight_grad = (
        lax.psum_scatter(
            query_weight_grad.astype(jnp.bfloat16), "ctx", scatter_dimension=0, tiled=True
        ).astype(jnp.float32),
        lax.psum_scatter(
            key_weight_grad.astype(jnp.bfloat16), "ctx", scatter_dimension=0, tiled=True
        ).astype(jnp.float32),
        lax.psum_scatter(
            value_weight_grad.astype(jnp.bfloat16), "ctx", scatter_dimension=0, tiled=True
        ).astype(jnp.float32),
        lax.psum_scatter(
            gate_weight_grad.astype(jnp.bfloat16), "ctx", scatter_dimension=0, tiled=True
        ).astype(jnp.float32),
        lax.psum_scatter(
            up_weight_grad.astype(jnp.bfloat16), "ctx", scatter_dimension=0, tiled=True
        ).astype(jnp.float32),
    )
    out_weight_grad, down_weight_grad = (
        lax.psum_scatter(
            out_weight_grad.astype(jnp.bfloat16), "ctx", scatter_dimension=1, tiled=True
        ).astype(jnp.float32),
        lax.psum_scatter(
            down_weight_grad.astype(jnp.bfloat16), "ctx", scatter_dimension=1, tiled=True
        ).astype(jnp.float32),
    )
    mixed = output.astype(jnp.bfloat16).reshape(seq_count, 2, 1, block_len, width)
    return (
        mixed,
        input_grad,
        norm_gain_grad,
        query_weight_grad,
        key_weight_grad,
        value_weight_grad,
        query_gain_grad,
        key_gain_grad,
        out_weight_grad,
        post_gain_grad,
        gate_weight_grad,
        up_weight_grad,
        down_weight_grad,
    )


def solution(mesh):
    in_specs = (
        P(None, None, "ctx", None, None),
        P(),
        P(None, "tp"),
        P(None, "tp"),
        P(None, "tp"),
        P(),
        P(),
        P("tp", None),
        P(),
        P(None, "tp"),
        P(None, "tp"),
        P("tp", None),
        P(None, None, "ctx", None, None),
    )
    out_specs = (
        P(None, None, "ctx", None, None),
        P(None, None, "ctx", None, None),
        P(),
        P("ctx", "tp"),
        P("ctx", "tp"),
        P("ctx", "tp"),
        P(),
        P(),
        P("tp", "ctx"),
        P(),
        P("ctx", "tp"),
        P("ctx", "tp"),
        P("tp", "ctx"),
    )
    return jax.shard_map(
        on_device, mesh=mesh, in_specs=in_specs, out_specs=out_specs, check_vma=False
    )
```

profile of v0, /device:TPU:0, one launch (start us, length us, event | category | flops | bytes accessed | tf_op | source)
XLA Modules:
  0.0 1213.1 jit_solution(15868584822241590967)
XLA Ops:
  10.0 1.9 convolution_convert_fusion.9
  11.9 1.8 copy.100
  29.1 1.8 broadcast_compare_fusion.1
  30.9 27.6 %all-gather.3.cloned.1.call-done = bf16[2,2,32,64,128]{4,3,1,0,2:T(8,128)(2,1)} async-done(((bf16[2,2,1,64,128]{4,3,1,0,2:T(8,128)(2,1)}), bf16[2,2,32,64,128]{4,3,1,0,2:T(8,128)(2,1)}) %all-gather.3.cloned.1.call-update) | async-done | bytes 2097168 | tf_op jit(solution)/shard_map/all_gather | solution.py:118
  58.5 3.2 fusion.96
  61.7 4.7 copy.99
  66.4 4.2 reshape.445
  70.6 33.5 %all-gather.5.cloned.1.call-done = bf16[2,2,32,64,128]{4,3,1,0,2:T(8,128)(2,1)} async-done(((bf16[2,2,1,64,128]{4,3,1,0,2:T(8,128)(2,1)}), bf16[2,2,32,64,128]{4,3,1,0,2:T(8,128)(2,1)}) %all-gather.5.cloned.1.call-update) | async-done | bytes 2097168 | tf_op jit(solution)/shard_map/all_gather | solution.py:117
  104.0 2.8 fusion.97
  106.8 3.8 copy.102
  110.6 3.3 reshape.444
  113.9 5.1 copy.106
  119.0 4.2 reshape.447
  123.2 4.7 copy.107
  127.9 4.3 reshape.446
  132.3 2.4 fusion.100
  149.9 41.1 %all-reduce.7.cloned.1.call-done = bf16[256,1024]{1,0:T(8,128)(2,1)} async-done(((bf16[256,1024]{1,0:T(8,128)(2,1)}), bf16[256,1024]{1,0:T(8,128)(2,1)}) %all-reduce.7.cloned.1.call-update) | async-done | bytes 524304 | tf_op jit(solution)/shard_map/psum | solution.py:161
  194.3 2.7 fusion.105
  198.0 2.1 multiply_convert_fusion.4
  206.2 40.4 %all-reduce.9.cloned.1.call-done = bf16[256,1024]{1,0:T(8,128)(2,1)} async-done(((bf16[256,1024]{1,0:T(8,128)(2,1)}), bf16[256,1024]{1,0:T(8,128)(2,1)}) %all-reduce.9.cloned.1.call-update) | async-done | bytes 524304 | tf_op jit(solution)/shard_map/psum | solution.py:183
  246.5 2.1 fusion.63
  252.1 3.7 multiply_reduce_fusion
  257.8 2.4 copy-done.4
  265.5 4.4 stack.19
  269.9 3.7 multiply_reduce_fusion.2
  275.6 2.4 copy-done.9
  283.4 4.2 stack.18
  287.6 5.1 pad_maximum_fusion
  292.7 5.9 copy.114
  298.7 3.3 convolution_bitcast_fusion.6
  302.1 2.1 fusion.20
  304.2 4.4 stack.21
  308.6 3.3 convolution_bitcast_fusion.4
  312.2 2.0 fusion.21
  314.2 4.3 stack.22
  318.5 5.2 pad_maximum_fusion.1
  323.7 5.9 copy.121
  329.7 3.2 convolution_multiply_fusion.5
  332.9 3.1 convolution_multiply_fusion.4
  340.6 1.8 multiply_reduce_fusion.5
  345.5 3.6 convolution_convert_fusion.1
  349.1 3.6 convolution_convert_fusion.2
  353.0 3.5 convolution_convert_fusion
  356.6 2.7 convolution_convert_fusion.5
  359.3 19.1 %reduce-scatter.10.cloned.1.call-done = bf16[2,2,1,64,128]{4,3,1,0,2:T(8,128)(2,1)} async-done(((bf16[2,2,32,64,128]{4,3,1,0,2:T(8,128)(2,1)}), bf16[2,2,1,64,128]{4,3,1,0,2:T(8,128)(2,1)}) %reduce-scatter.10.cloned.1.call-update) | async-done | bytes 65552 | tf_op jit(solution)/shard_map/reduce_scatter | solution.py:244
  378.4 1.7 reshape.442
  380.2 2.1 fusion.98
  382.3 1.7 copy.143
  387.4 72.6 %reduce-scatter.12.cloned.1.call-done = bf16[2,2,1,64,128]{4,3,1,0,2:T(8,128)(2,1)} async-done(((bf16[2,2,32,64,128]{4,3,1,0,2:T(8,128)(2,1)}), bf16[2,2,1,64,128]{4,3,1,0,2:T(8,128)(2,1)}) %reduce-scatter.12.cloned.1.call-update) | async-done | bytes 65552 | tf_op jit(solution)/shard_map/reduce_scatter | solution.py:252
  460.0 1.9 fusion.49
  462.0 1.9 convolution_convert_fusion.7
  463.9 2.4 fusion.107
  467.7 2.5 fusion.43
  470.3 69.6 %reduce-scatter.20.cloned.1.call-done = bf16[256,32]{0,1:T(8,128)(2,1)} async-done(((bf16[256,1024]{0,1:T(8,128)(2,1)}), bf16[256,32]{0,1:T(8,128)(2,1)}) %reduce-scatter.20.cloned.1.call-update) | async-done | bytes 16400 | tf_op jit(solution)/shard_map/reduce_scatter | solution.py:308
  541.3 78.5 %reduce-scatter.14.cloned.1.call-done = bf16[32,256]{1,0:T(8,128)(2,1)} async-done(((bf16[1024,256]{1,0:T(8,128)(2,1)}), bf16[32,256]{1,0:T(8,128)(2,1)}) %reduce-scatter.14.cloned.1.call-update) | async-done | bytes 16400 | tf_op jit(solution)/shard_map/reduce_scatter | solution.py:291
  621.1 80.8 %reduce-scatter.24.cloned.1.call-done = bf16[32,1152]{1,0:T(8,128)(2,1)} async-done(((bf16[1024,1152]{1,0:T(8,128)(2,1)}), bf16[32,1152]{1,0:T(8,128)(2,1)}) %reduce-scatter.24.cloned.1.call-update) | async-done | bytes 73744 | tf_op jit(solution)/shard_map/reduce_scatter | solution.py:303
  703.5 80.9 %reduce-scatter.22.cloned.1.call-done = bf16[32,1152]{1,0:T(8,128)(2,1)} async-done(((bf16[1024,1152]{1,0:T(8,128)(2,1)}), bf16[32,1152]{1,0:T(8,128)(2,1)}) %reduce-scatter.22.cloned.1.call-update) | async-done | bytes 73744 | tf_op jit(solution)/shard_map/reduce_scatter | solution.py:300
  785.9 80.6 %reduce-scatter.26.cloned.1.call-done = bf16[1152,32]{0,1:T(8,128)(2,1)} async-done(((bf16[1152,1024]{0,1:T(8,128)(2,1)}), bf16[1152,32]{0,1:T(8,128)(2,1)}) %reduce-scatter.26.cloned.1.call-update) | async-done | bytes 73744 | tf_op jit(solution)/shard_map/reduce_scatter | solution.py:311
  868.1 10.6 all-reduce.1
  878.7 67.9 %reduce-scatter.18.cloned.1.call-done = bf16[32,128]{1,0:T(8,128)(2,1)} async-done(((bf16[1024,128]{1,0:T(8,128)(2,1)}), bf16[32,128]{1,0:T(8,128)(2,1)}) %reduce-scatter.18.cloned.1.call-update) | async-done | bytes 8208 | tf_op jit(solution)/shard_map/reduce_scatter | solution.py:297
  947.9 78.8 %reduce-scatter.16.cloned.1.call-done = bf16[32,128]{1,0:T(8,128)(2,1)} async-done(((bf16[1024,128]{1,0:T(8,128)(2,1)}), bf16[32,128]{1,0:T(8,128)(2,1)}) %reduce-scatter.16.cloned.1.call-update) | async-done | bytes 8208 | tf_op jit(solution)/shard_map/reduce_scatter | solution.py:294
  1028.0 46.8 %all-reduce.11.cloned.1.call-done = (bf16[256,1024]{1,0:T(8,128)(2,1)}, bf16[256,1024]{1,0:T(8,128)(2,1)}) async-done(((bf16[256,1024]{1,0:T(8,128)(2,1)}, bf16[256,1024]{1,0:T(8,128)(2,1)}), (bf16[256,1024]{1,0:T(8,128)(2,1)}, bf16[256,1024]{1,0:T(8,128)(2,1)})) %all-reduce.11.cloned.1.call-update) | async-done | bytes 1048592 | tf_op jit(solution)/shard_map/psum | solution.py:170
  1076.2 127.0 %all-reduce = (f32[1024]{0:T(1024)}, f32[64]{0:T(128)}, f32[64]{0:T(128)}, f32[1024]{0:T(1024)}) all-reduce(f32[1024]{0:T(1024)S(1)} %get-tuple-element.67, bf16[64]{0:T(256)(128)(2,1)S(1)} %get-tuple-element.77, bf16[64]{0:T(256)(128)(2,1)S(1)} %get-tuple-element.78, f32[1024]{0:T(1024)S(1)} %copy-done.73), channel_id=1, replica_groups=mesh['ctx'=32,'tp'=4] {'ctx'}, use_global_device_ids=true, to_apply=%region_27.28 | all-reduce | flops 2176 | bytes 17152 | tf_op jit(solution)/shard_map/psum | solution.py:286
  1203.2 3.0 fusion.58
  (291 shorter events, 85.7 us)
Async XLA Ops:
  7.2 190.8 %copy-start = (bf16[1152,1024]{1,0:T(8,128)(2,1)S(1)}, bf16[1152,1024]{1,0:T(8,128)(2,1)}, u32[]{:S(2)}) copy-start(bf16[1152,1024]{1,0:T(8,128)(2,1)} %param.24) | copy-start | bytes 7077892
  7.2 9.6 copy-start.81
  7.2 15.7 %copy-start.39 = (bf16[1024,256]{1,0:T(8,128)(2,1)S(1)}, bf16[1024,256]{1,0:T(8,128)(2,1)}, u32[]{:S(2)}) copy-start(bf16[1024,256]{1,0:T(8,128)(2,1)} %param.15) | copy-start | bytes 1572868
  7.2 51.3 %all-gather.3.cloned.1.call-start = ((), (), s32[]{:S(2)}) async-start(), calls=%async_computation.9 | async-start | bytes 2162688 | tf_op jit(solution)/shard_map/all_gather | solution.py:118
  8.7 5.1 copy-start.74
  11.9 92.1 %all-gather.5.cloned.1.call-start = ((), (), s32[]{:S(2)}) async-start(), calls=%async_computation.10 | async-start | bytes 2162688 | tf_op jit(solution)/shard_map/all_gather | solution.py:117
  15.1 46.6 %copy-start.21 = (bf16[2,2,1,64,1024]{4,3,2,1,0:T(8,128)(2,1)}, bf16[2,2,1,64,1024]{4,3,2,1,0:T(8,128)(2,1)S(1)}, u32[]{:S(2)}) copy-start(bf16[2,2,1,64,1024]{4,3,2,1,0:T(8,128)(2,1)S(1)} %fusion.88) | copy-start | bytes 1572868
  21.4 169.7 %all-reduce.7.cloned.1.call-start = ((), (), s32[]{:S(2)}) async-start(), calls=%async_computation.11 | async-start | bytes 1048576 | tf_op jit(solution)/shard_map/psum | solution.py:161
  113.9 27.6 %copy-start.12 = (bf16[4096,2,64,1]{0,2,1,3:T(8,128)(2,1)}, bf16[4096,2,64,1]{0,2,1,3:T(8,128)(2,1)S(1)}, u32[]{:S(2)}) copy-start(bf16[4096,2,64,1]{0,2,1,3:T(8,128)(2,1)S(1)} %reshape.444) | copy-start | bytes 3145732
  132.3 3.1 copy-start.30
  136.7 10.2 copy-start.56
  140.5 6.5 copy-start.58
  142.5 3.0 copy-start.8
  142.5 3.0 copy-start.71
  145.6 45.4 %copy-start.11 = (bf16[2,2,1,64,1024]{4,3,2,1,0:T(8,128)(2,1)S(1)}, bf16[2,2,1,64,1024]{4,3,2,1,0:T(8,128)(2,1)}, u32[]{:S(2)}) copy-start(bf16[2,2,1,64,1024]{4,3,2,1,0:T(8,128)(2,1)} %param.13) | copy-start | bytes 1572868
  145.6 47.5 %copy-start.65 = (f32[1024]{0:T(1024)S(1)}, f32[1024]{0:T(1024)}, u32[]{:S(2)}) copy-start(f32[1024]{0:T(1024)} %param.21) | copy-start | bytes 12292
  148.7 97.8 %all-reduce.9.cloned.1.call-start = ((), (), s32[]{:S(2)}) async-start(), calls=%async_computation.12 | async-start | bytes 1048576 | tf_op jit(solution)/shard_map/psum | solution.py:183
  191.0 6.0 copy-start.32
  194.3 2.7 copy-start.27
  194.3 3.6 copy-start.42
  197.9 3.2 copy-start.33
  200.1 46.5 %copy-start.25 = (bf16[256,1024]{1,0:T(8,128)(2,1)S(1)}, bf16[256,1024]{1,0:T(8,128)(2,1)}, u32[]{:S(2)}) copy-start(bf16[256,1024]{1,0:T(8,128)(2,1)} %all-reduce.7.cloned.1.call-done) | copy-start | bytes 1572868
  202.8 175.6 %reduce-scatter.10.cloned.1.call-start = ((), (), s32[]{:S(2)}) async-start(), calls=%async_computation.13 | async-start | bytes 2162688 | tf_op jit(solution)/shard_map/reduce_scatter | solution.py:244
  246.5 4.7 copy-start.41
  252.1 3.8 copy-start.2
  257.3 5.4 copy-start.15
  257.3 2.9 copy-start.4
  257.3 2.9 copy-start.68
  261.3 2.7 copy-start.55
  269.9 3.7 copy-start.7
  275.1 4.1 copy-start.16
  275.1 2.9 copy-start.9
  275.1 2.9 copy-start.69
  279.2 2.7 copy-start.53
  298.6 161.4 %reduce-scatter.12.cloned.1.call-start = ((), (), s32[]{:S(2)}) async-start(), calls=%async_computation.14 | async-start | bytes 2162688 | tf_op jit(solution)/shard_map/reduce_scatter | solution.py:252
  298.7 3.5 copy-start.10
  308.6 3.6 copy-start.5
  329.6 210.3 %reduce-scatter.20.cloned.1.call-start = ((), (), s32[]{:S(2)}) async-start(), calls=%async_computation.18 | async-start | bytes 540672 | tf_op jit(solution)/shard_map/reduce_scatter | solution.py:308
  329.6 6.3 copy-start.13
  329.6 6.3 copy-start.20
  329.7 7.5 copy-start.17
  336.0 2.5 copy-start.46
  336.0 2.5 copy-start.48
  336.0 3.3 copy-start.24
  336.0 3.3 copy-start.57
  336.0 3.2 copy-start.59
  336.0 3.2 copy-start.61
  336.1 3.2 copy-start.63
  337.2 3.4 copy-start.83
  337.2 7.0 copy-start.22
  340.6 279.2 %reduce-scatter.14.cloned.1.call-start = ((), (), s32[]{:S(2)}) async-start(), calls=%async_computation.15 | async-start | bytes 540672 | tf_op jit(solution)/shard_map/reduce_scatter | solution.py:291
  345.4 356.5 %reduce-scatter.24.cloned.1.call-start = ((), (), s32[]{:S(2)}) async-start(), calls=%async_computation.20 | async-start | bytes 2433024 | tf_op jit(solution)/shard_map/reduce_scatter | solution.py:303
  349.0 435.4 %reduce-scatter.22.cloned.1.call-start = ((), (), s32[]{:S(2)}) async-start(), calls=%async_computation.19 | async-start | bytes 2433024 | tf_op jit(solution)/shard_map/reduce_scatter | solution.py:300
  352.7 513.9 %reduce-scatter.26.cloned.1.call-start = ((), (), s32[]{:S(2)}) async-start(), calls=%async_computation.21 | async-start | bytes 2433024 | tf_op jit(solution)/shard_map/reduce_scatter | solution.py:311
  356.5 30.0 %copy-start.67 = (f32[256,2]{0,1:T(2,128)S(1)}, f32[256,2]{0,1:T(2,128)}, u32[]{:S(2)}) copy-start(f32[256,2]{0,1:T(2,128)} %copy-done.66) | copy-start | bytes 6148
  356.5 30.0 %copy-start.82 = (f32[64]{0:T(128)S(1)}, f32[64]{0:T(128)}, u32[]{:S(2)}) copy-start(f32[64]{0:T(128)} %param.19) | copy-start | bytes 772
  356.6 590.0 %reduce-scatter.18.cloned.1.call-start = ((), (), s32[]{:S(2)}) async-start(), calls=%async_computation.17 | async-start | bytes 270336 | tf_op jit(solution)/shard_map/reduce_scatter | solution.py:297
  387.4 80.3 %copy-start.44 = (bf16[256,4,64]{0,2,1:T(8,128)(2,1)S(1)}, bf16[256,4,64]{0,2,1:T(8,128)(2,1)}, u32[]{:S(2)}) copy-start(bf16[256,4,64]{0,2,1:T(8,128)(2,1)} %copy-done.43) | copy-start | bytes 393220
  462.0 564.7 %reduce-scatter.16.cloned.1.call-start = ((), (), s32[]{:S(2)}) async-start(), calls=%async_computation.16 | async-start | bytes 270336 | tf_op jit(solution)/shard_map/reduce_scatter | solution.py:294
  463.9 610.9 %copy-start.64 = (f32[1024]{0:T(1024)S(1)}, f32[1024]{0:T(1024)}, u32[]{:S(2)}) copy-start(f32[1024]{0:T(1024)} %param.14) | copy-start | bytes 12292
  463.9 610.9 %copy-start.75 = (f32[256]{0:T(256)S(1)}, f32[256]{0:T(256)}, u32[]{:S(2)}) copy-start(f32[256]{0:T(256)} %copy-done.74) | copy-start | bytes 3076
  466.3 609.9 %copy-start.73 = (f32[1024]{0:T(1024)S(1)}, f32[1024]{0:T(1024)}, u32[]{:S(2)}) copy-start(f32[1024]{0:T(1024)} %get-tuple-element.65) | copy-start | bytes 12292
  466.3 736.9 %copy-start.26 = (bf16[256,1024]{1,0:T(8,128)(2,1)S(1)}, bf16[256,1024]{1,0:T(8,128)(2,1)}, u32[]{:S(2)}) copy-start(bf16[256,1024]{1,0:T(8,128)(2,1)} %all-reduce.7.cloned.1.call-done) | copy-start | bytes 1572868
  466.3 608.4 %all-reduce.11.cloned.1.call-start = ((), (), s32[]{:S(2)}) async-start(), calls=%async_computation.22 | async-start | bytes 2097152 | tf_op jit(solution)/shard_map/psum | solution.py:170
  (36 other events, 50.4 us)
Sparse Core Ops, SparseCore 0:
  12.0 46.4 all-gather.2
  60.8 43.2 all-gather.4
  148.9 42.1 all-reduce.6
  203.0 43.5 all-reduce.8
  298.7 79.6 reduce-scatter.9
  381.8 78.1 reduce-scatter.11
  463.5 76.3 reduce-scatter.19
  543.4 76.3 reduce-scatter.13
  623.4 78.4 reduce-scatter.23
  705.7 78.6 reduce-scatter.21
  788.0 78.5 reduce-scatter.25
  870.3 76.2 reduce-scatter.17
  950.4 76.2 reduce-scatter.15
  1029.7 45.0 all-reduce.10
where the time goes:
time: 1220 us; the launch traced here: 1210 us
  waiting for transfers between devices  819 us (67%)
  blocking collectives  138 us (11%)
  local copies, waits for them, and re-layouts  97.9 us (8%)
  matrix products  83.6 us (7%)
  other arithmetic  58.8 us (5%)
  between operations  15.5 us (1%)
    psum x1, blocking collectives, on_device(): lax.psum((jnp.sum(norm_gain_term, 0), jnp.sum(post_gain_term, 0), query_g...  127 us
    reduce_scatter x1, waiting for transfers between devices, on_device(): lax.psum_scatter(gate_weight_grad.astype(jnp.bfloat16), 'ctx', scatter_di...  80.9 us
    reduce_scatter x1, waiting for transfers between devices, on_device(): lax.psum_scatter(up_weight_grad.astype(jnp.bfloat16), 'ctx', scatter_dime...  80.8 us
    reduce_scatter x1, waiting for transfers between devices, on_device(): lax.psum_scatter(down_weight_grad.astype(jnp.bfloat16), 'ctx', scatter_di...  80.6 us
    reduce_scatter x1, waiting for transfers between devices, on_device(): lax.psum_scatter(key_weight_grad.astype(jnp.bfloat16), 'ctx', scatter_dim...  78.8 us
    reduce_scatter x1, waiting for transfers between devices, on_device(): lax.psum_scatter(query_weight_grad.astype(jnp.bfloat16), 'ctx', scatter_d...  78.5 us
    reduce_scatter x1, waiting for transfers between devices, on_device(): lax.psum_scatter(jnp.stack(value_grad_list, 0).reshape(seq_count, 2, ctx_...  72.6 us
    reduce_scatter x1, waiting for transfers between devices, on_device(): lax.psum_scatter(out_weight_grad.astype(jnp.bfloat16), 'ctx', scatter_dim...  69.6 us
  transfers between devices with their start and end apart: 14, of which 14 were waited for; matrix products, arithmetic and copies ran while one was open for 10% of the time, Pallas kernels for 0%

commit v1 on v0

v1 whole, which is shorter than its diff:
```python
import jax
import jax.numpy as jnp
import numpy as np
from jax import lax
from jax.experimental import pallas as pl
from jax.experimental.pallas import tpu as pltpu
from jax.sharding import PartitionSpec as P

HD = 64
EPS = 1e-05
ROPE_BASE = 1000000.0
BF = jnp.bfloat16
F32 = jnp.float32
MESH = pl.DeviceIdType.MESH
FF = 1152
GX = 3 * FF
G2X = 768

NN = (((1,), (0,)), ((), ()))
NT = (((1,), (1,)), ((), ()))
TN = (((0,), (0,)), ((), ()))


def dot(a, b, dims=NN):
    return lax.dot_general(a, b, dims, preferred_element_type=F32)


def rope_constants():
    freq = ROPE_BASE ** (-np.arange(0, HD, 2) / HD)
    freq = np.tile(freq, 4)[None, :]
    rows = np.arange(64)[:, None] * freq
    blocks = np.arange(64)[:, None] * 64.0 * freq
    return [f(a).astype(np.float32) for a in (rows, blocks) for f in (np.cos, np.sin)]


def lanes(shape):
    return lax.broadcasted_iota(jnp.int32, shape, len(shape) - 1)


def swap_halves(u):
    return jnp.where(lanes(u.shape) % 64 < 32, pltpu.roll(u, 96, 1), pltpu.roll(u, 32, 1))


def head_mean(u):
    low = lanes(u.shape) < 64
    first = jnp.sum(jnp.where(low, u, 0.0), -1, keepdims=True)
    second = jnp.sum(jnp.where(low, 0.0, u), -1, keepdims=True)
    return jnp.where(low, first, second) * (1.0 / 64)


def head_norm(u, gain):
    return u * lax.rsqrt(head_mean(u * u) + EPS) * gain


def head_norm_back(u, gain, grads):
    inv = lax.rsqrt(head_mean(u * u) + EPS)
    scaled = grads * gain
    back = inv * (scaled - u * (inv * inv) * head_mean(scaled * u))
    return back, grads * u * inv


def row_inverse(u):
    return lax.rsqrt(jnp.mean(u * u, -1, keepdims=True) + EPS)


def row_norm_back(u, gain, grads):
    inv = row_inverse(u)
    scaled = grads * gain
    back = inv * (scaled - u * (inv * inv) * jnp.mean(scaled * u, -1, keepdims=True))
    return back, grads * u * inv


def to_diagonal(part, kv, ref):
    low = lanes((64, 128)) < 64
    for s in range(2):
        for h in range(2):
            a = part[(s * 2 + h) * 64 : (s * 2 + h + 1) * 64]
            b = pltpu.roll(a, 64, 1)
            first, second = (a, b) if kv == 0 else (b, a)
            keep = low if kv == 0 else jnp.logical_not(low)
            at = h * 256 + kv * 128
            ref[s, at : at + 64, :] = jnp.where(keep, first, 0.0).astype(ref.dtype)
            ref[s, at + 64 : at + 128, :] = jnp.where(keep, second, 0.0).astype(ref.dtype)


def from_diagonal(rows, kv):
    low = lanes((64, 128)) < 64
    a = rows[kv * 128 : kv * 128 + 64]
    b = rows[kv * 128 + 64 : kv * 128 + 128]
    if kv == 0:
        return jnp.where(low, a, pltpu.roll(b, 64, 1))
    return jnp.where(low, pltpu.roll(a, 64, 1), b)


def kernel(
    x, ng, wq, wk, wv, qg, kg, wo_in, pg, wg_in, wu_in, wd_in, gy, cr, sr, cb, sb,
    mixed_out, xgrad_out, gains_out, gate_out, up_out, down_out, attn_out,
    wg, wu, wd, wo_all, nrm, kv_all, kp, qp, ct, st_, qbd, dobd, ot, stats, att_all,
    mid, post, hid, gg, ug, pp, ppb, mpb, ipb, xr, ml, mgr, mixed_s, xg_s, dq, dql, kvl,
    g1, r1, ra1, rb1, dkv, r0, ra0, rb0, g2, r2, ra2, rb2, gv, gr,
    loc, kss, krs, xss, xrs, s1, q1, s0, q0, s2, q2, gss, grs,
):
    c = lax.axis_index("ctx")
    t = lax.axis_index("tp")
    cy = lax.div(c, 8)
    cz = lax.rem(lax.div(c, 2), 4)
    ck = lax.rem(c, 2)
    sib = 1 - ck

    def off(v, d):
        return lax.rem(v + d + 4, 4)

    def at_y(d):
        return ((off(cy, d) * 4 + cz) * 2 + ck, t)

    def at_z(d):
        return ((cy * 4 + off(cz, d)) * 2 + ck, t)

    def at_x(d):
        return (c, off(t, d))

    at_k = ((cy * 4 + cz) * 2 + sib, t)
    order = (1, 3, 2)

    barrier = pltpu.get_barrier_semaphore()
    for d in order:
        for peer in (at_x(d), at_y(d), at_z(d)):
            pl.semaphore_signal(barrier, inc=1, device_id=peer, device_id_type=MESH)
    pl.semaphore_signal(barrier, inc=1, device_id=at_k, device_id_type=MESH)

    locals_ = []
    for n, (src, dst) in enumerate(
        ((wo_in, wo_all.at[t]), (wg_in, wg), (wu_in, wu), (wd_in, wd))
    ):
        cp = pltpu.make_async_copy(src, dst, loc.at[n])
        cp.start()
        locals_.append(cp)

    sent = []

    def remote(src, dst, ssem, rsem, peer):
        cp = pltpu.make_async_remote_copy(
            src_ref=src, dst_ref=dst, send_sem=ssem, recv_sem=rsem, device_id=peer, device_id_type=MESH
        )
        cp.start()
        sent.append(cp)
        return cp

    xf = x[...].astype(F32)
    nrm[...] = (xf * row_inverse(xf) * ng[...]).astype(BF)
    lane64 = lanes((64, 128))
    sign = jnp.where(lane64 % 64 < 32, -1.0, 1.0)
    for h in range(2):
        place = c if h == 0 else 63 - c
        cos_b, sin_b = cb[pl.ds(place, 1), :], sb[pl.ds(place, 1), :]
        cos_h = cos_b * cr[...] - sin_b * sr[...]
        sin_h = (sin_b * cr[...] + cos_b * sr[...]) * sign
        for s in range(2):
            ct[pl.ds((s * 2 + h) * 64, 64), :] = cos_h
            st_[pl.ds((s * 2 + h) * 64, 64), :] = sin_h

    def rotate(u):
        return u * ct[...] + swap_halves(u) * st_[...]

    def rotate_back(u):
        return u * ct[...] - swap_halves(u) * st_[...]

    kproj = dot(nrm[...], wk[...])
    kp[...] = kproj
    kv_all[0, c] = rotate(head_norm(kproj, kg[...])).astype(BF)
    kv_all[1, c] = dot(nrm[...], wv[...]).astype(BF)

    pl.semaphore_wait(barrier, 10)

    arrive = {}

    def pass_on(kind, dy, dz, axis, d):
        source = (off(cy, -dy) * 4 + off(cz, -dz)) * 2 + ck
        if axis == "y":
            key, peer = (dy + d, dz, 0), at_y(d)
        elif axis == "z":
            key, peer = (dy, dz + d, 0), at_z(d)
        else:
            key, peer = (dy, dz, 1), at_k
        n = (key[0] * 4 + key[1]) * 2 + key[2]
        ref = kv_all.at[kind, source]
        arrive[kind, key] = remote(ref, ref, kss.at[kind, n], krs.at[kind, n], peer)

    for d in order:
        pass_on(0, 0, 0, "y", d)
        pass_on(1, 0, 0, "z", d)
    for kind in range(2):
        pass_on(kind, 0, 0, "k", 1)
    for d in order:
        pass_on(0, 0, 0, "z", d)
        pass_on(1, 0, 0, "y", d)

    locals_[0].wait()
    wo_c = [
        remote(wo_all.at[t], wo_all.at[t], xss.at[0, d - 1], xrs.at[0, d - 1], at_x(d)) for d in order
    ]

    for kv in range(2):
        proj = dot(nrm[...], wq[:, kv * 128 : (kv + 1) * 128])
        qp[kv] = proj
        to_diagonal(rotate(head_norm(proj, qg[...])).astype(BF).astype(F32) * 0.125, kv, qbd)

    for d in order:
        arrive[0, (d, 0, 0)].wait_recv()
        for e in order:
            pass_on(0, d, 0, "z", e)
        pass_on(0, d, 0, "k", 1)
        arrive[1, (0, d, 0)].wait_recv()
        for e in order:
            pass_on(1, 0, d, "y", e)
        pass_on(1, 0, d, "k", 1)
    for a in (0, 1, 3, 2):
        for b in order:
            arrive[0, (a, b, 0)].wait_recv()
            pass_on(0, a, b, "k", 1)
            arrive[1, (b, a, 0)].wait_recv()
            pass_on(1, b, a, "k", 1)
    for kind in range(2):
        for dy in range(4):
            for dz in range(4):
                arrive[kind, (dy, dz, 1)].wait_recv()

    own_chunk = cy

    def chunk(kind, j, s, kh):
        return kv_all[kind, pl.ds(j * 8, 8), pl.ds((s * 2 + kh) * 64, 64), :].reshape(512, 128)

    def visible_front(j, width):
        keys = j * 512 + lax.broadcasted_iota(jnp.int32, (512, width), 0)
        lane = lax.broadcasted_iota(jnp.int32, (512, width), 1)
        return (keys <= c * 64 + lane % 64) | (lane >= 256)

    def visible_back(j):
        keys = lax.broadcasted_iota(jnp.int32, (512, 256), 0)
        lane = lax.broadcasted_iota(jnp.int32, (512, 256), 1)
        return keys % 64 - 64 * (j * 8 + keys // 64) <= lane % 64 - 64 * c

    def forward_step(j, carry, h, kh, mask):
        out = []
        seen = mask(j) if mask is not None else None
        for s in range(2):
            m, l = carry[s]
            scores = dot(chunk(0, j, s, kh), qbd[s, h * 256 : (h + 1) * 256, :], NT)
            if seen is not None:
                scores = jnp.where(seen, scores, -1e30)
            new = jnp.maximum(m, jnp.max(scores, 0, keepdims=True))
            p = jnp.exp(scores - new)
            scale = jnp.exp(m - new)
            l = l * scale + jnp.sum(p, 0, keepdims=True)
            ot[s, :, h * 256 : (h + 1) * 256] = ot[s, :, h * 256 : (h + 1) * 256] * scale + dot(
                chunk(1, j, s, kh), p.astype(BF), TN
            )
            out.append((new, l))
        return tuple(out)

    ot[...] = jnp.zeros_like(ot)
    start = tuple((jnp.full((1, 256), -1e30, F32), jnp.zeros((1, 256), F32)) for _ in range(2))
    totals = [None, None]
    totals[0] = lax.fori_loop(
        0, own_chunk + 1, lambda j, v: forward_step(j, v, 0, 0, lambda n: visible_front(n, 256)), start
    )
    run = lax.fori_loop(0, 4, lambda j, v: forward_step(j, v, 1, 0, None), start)
    totals[1] = lax.fori_loop(
        own_chunk, 4, lambda j, v: forward_step(j, v, 1, 1, visible_back), run
    )
    for s in range(2):
        for h in range(2):
            m, l = totals[h][s]
            cols = slice(h * 256, (h + 1) * 256)
            o = ot[s, :, cols] / l
            ot[s, :, cols] = o
            stats[s, 0:1, cols] = m + jnp.log(l)
            rows = o.T
            for kv in range(2):
                att_all[t, pl.ds((s * 2 + h) * 64, 64), kv * 128 : (kv + 1) * 128] = from_diagonal(
                    rows, kv
                ).astype(BF)

    att_c = [
        remote(att_all.at[t], att_all.at[t], xss.at[1, d - 1], xrs.at[1, d - 1], at_x(d)) for d in order
    ]
    for cp in locals_[1:]:
        cp.wait()
    for cp in wo_c:
        cp.wait_recv()
    for cp in att_c:
        cp.wait_recv()

    branch = dot(att_all[0], wo_all[0])
    for n in range(1, 4):
        branch = branch + dot(att_all[n], wo_all[n])
    mid[...] = x[...].astype(F32) + branch
    post[...] = (mid[...] * row_inverse(mid[...]) * pg[...]).astype(BF)

    pp[...] = jnp.zeros_like(pp)

    def mlp_step(n, _):
        cols = pl.ds(pl.multiple_of(n * 384, 128), 384)
        g = dot(post[...], wg[:, cols])
        u = dot(post[...], wu[:, cols])
        hgrad = dot(gy[...], wd[cols, :], NT)
        sg = 1.0 / (1.0 + jnp.exp(-g))
        silu = g * sg
        hid[:, cols] = (silu * u).astype(BF)
        a = (hgrad * u * sg * (1.0 + g * (1.0 - sg))).astype(BF)
        b = (hgrad * silu).astype(BF)
        gg[:, cols] = a
        ug[:, cols] = b
        pp[...] += dot(a, wg[:, cols], NT) + dot(b, wu[:, cols], NT)
        return 0

    lax.fori_loop(0, 3, mlp_step, 0)

    def rows_of(n):
        return pl.ds(pl.multiple_of(n * 64, 64), 64)

    def scatter_x(src, n):
        return [
            remote(src.at[rows_of(off(t, d))], xr.at[n - 2, d - 1], xss.at[n, d - 1], xrs.at[n, d - 1], at_x(d))
            for d in order
        ]

    def collect_x(src, n, copies):
        total = src[rows_of(t), :].astype(F32)
        for cp in copies:
            cp.wait_recv()
        for d in range(3):
            total = total + xr[n - 2, d].astype(F32)
        return total

    def spread_x(buf, n):
        return [
            remote(buf.at[rows_of(t)], buf.at[rows_of(t)], xss.at[n, d - 1], xrs.at[n, d - 1], at_x(d))
            for d in order
        ]

    ppb[...] = pp[...].astype(BF)
    post_c = scatter_x(ppb, 2)
    mpb[...] = dot(hid[...], wd[...]).astype(BF)
    mlp_c = scatter_x(mpb, 3)

    def core_stage(g, r, ss, qs, y):
        return remote(g.at[y, :, sib], r.at[y], ss.at[y], qs.at[y], at_k)

    def core_sum(g, r, y, copy):
        copy.wait_recv()

        def add(z, _):
            r[y, z] = (g[y, z, ck].astype(F32) + r[y, z].astype(F32)).astype(BF)
            return 0

        lax.fori_loop(0, 4, add, 0)

    def first_stage(r, ra, ss, qs):
        out = []
        for d in order:
            out.append(remote(r.at[off(cy, d), :, 0], ra.at[0, d - 1], ss.at[3 + d], qs.at[3 + d], at_y(d)))
            out.append(remote(r.at[:, off(cz, d), 1], ra.at[1, d - 1], ss.at[6 + d], qs.at[6 + d], at_z(d)))
        return out

    def first_sum(r, ra, copies):
        for cp in copies:
            cp.wait_recv()

        def add(n, _):
            for half, at in ((0, (cy, n)), (1, (n, cz))):
                total = r[at[0], at[1], half].astype(F32)
                for d in range(3):
                    total = total + ra[half, d, n].astype(F32)
                r[at[0], at[1], half] = total.astype(BF)
            return 0

        lax.fori_loop(0, 4, add, 0)

    def second_stage(r, rb, ss, qs):
        out = []
        for d in order:
            out.append(remote(r.at[cy, off(cz, d), 0], rb.at[0, d - 1], ss.at[9 + d], qs.at[9 + d], at_z(d)))
            out.append(remote(r.at[off(cy, d), cz, 1], rb.at[1, d - 1], ss.at[12 + d], qs.at[12 + d], at_y(d)))
        return out

    def second_sum(r, rb, copies):
        for cp in copies:
            cp.wait_recv()
        out = []
        for half in range(2):
            total = r[cy, cz, half].astype(F32)
            for d in range(3):
                total = total + rb[half, d].astype(F32)
            out.append(total)
        return out

    core1 = []
    for y in range(4):
        cols = slice(y * 256, (y + 1) * 256)
        for n, (a, b) in enumerate(((post, gg), (post, ug), (gy, hid))):
            part = dot(a[:, cols], b[...], TN).astype(BF)
            g1[y, :, :, :, :, n * FF : (n + 1) * FF] = part.reshape(4, 2, 2, 16, FF)
        core1.append(core_stage(g1, r1, s1, q1, y))

    post_grad = collect_x(ppb, 2, post_c)
    back, post_gain_term = row_norm_back(mid[rows_of(t), :], pg[...], post_grad)
    mgr[...] = gy[rows_of(t), :].astype(F32) + back
    ml[rows_of(t), :] = mgr[...].astype(BF)
    ml_c = spread_x(ml, 4)
    gv[0, 1:2, :] = jnp.sum(post_gain_term, 0, keepdims=True)

    mixed_s[rows_of(t), :] = (mid[rows_of(t), :] + collect_x(mpb, 3, mlp_c)).astype(BF)
    mixed_c = spread_x(mixed_s, 5)

    for y in range(4):
        core_sum(g1, r1, y, core1[y])
    first1 = first_stage(r1, ra1, s1, q1)

    for cp in ml_c:
        cp.wait_recv()

    ag = dot(ml[...], wo_all[t], NT).astype(BF).astype(F32)
    for kv in range(2):
        to_diagonal(ag[:, kv * 128 : (kv + 1) * 128], kv, dobd)
    for s in range(2):
        stats[s, 1:2, :] = jnp.sum(dobd[s].astype(F32).T * ot[s], 0, keepdims=True)
    dq[...] = jnp.zeros_like(dq)

    def back_step(j, s, kh, first, mask):
        at = slice(first, 512)
        kc, vc = chunk(0, j, s, kh), chunk(1, j, s, kh)
        q, do = qbd[s, at, :], dobd[s, at, :]
        p = jnp.exp(dot(kc, q, NT) - stats[s, 0:1, at])
        if mask is not None:
            p = jnp.where(mask(j), p, 0.0)
        ds = (p * (dot(vc, do, NT) - stats[s, 1:2, at])).astype(BF)
        where = pl.ds((s * 2 + kh) * 64, 64)
        dkv[j, :, :, 1, where, :] = dot(p.astype(BF), do).astype(BF).reshape(4, 2, 64, 128)
        dkv[j, :, :, 0, where, :] = dot(ds, q).astype(BF).reshape(4, 2, 64, 128)
        dq[s, at, :] += dot(ds, kc, TN)

    def front_both(j, _):
        for s in range(2):
            back_step(j, s, 0, 0, lambda n: visible_front(n, 512))
        return 0

    def front_one(j, _):
        for s in range(2):
            back_step(j, s, 0, 256, None)
        return 0

    def behind_one(j, _):
        for s in range(2):
            back_step(j, s, 1, 256, visible_back)
        return 0

    def behind_none(j, _):
        for s in range(2):
            for kind in range(2):
                dkv[j, :, :, kind, pl.ds((s * 2 + 1) * 64, 64), :] = jnp.zeros((4, 2, 64, 128), BF)
        return 0

    lax.fori_loop(0, own_chunk, behind_none, 0)
    lax.fori_loop(0, own_chunk + 1, front_both, 0)
    lax.fori_loop(own_chunk + 1, 4, front_one, 0)
    lax.fori_loop(own_chunk, 4, behind_one, 0)

    core0 = [core_stage(dkv, r0, s0, q0, y) for y in range(4)]

    query_gain_term = jnp.zeros((1, 128), F32)
    for kv in range(2):
        parts = [
            from_diagonal(dq[s, h * 256 : (h + 1) * 256, :], kv) for s in range(2) for h in range(2)
        ]
        grads = rotate_back(jnp.concatenate(parts, 0) * 0.125)
        back, term = head_norm_back(qp[kv], qg[...], grads)
        dql[:, kv * 128 : (kv + 1) * 128] = back.astype(BF)
        query_gain_term = query_gain_term + jnp.sum(term, 0, keepdims=True)

    for y in range(4):
        core_sum(dkv, r0, y, core0[y])
    first0 = first_stage(r0, ra0, s0, q0)

    first_sum(r1, ra1, first1)
    second1 = second_stage(r1, rb1, s1, q1)

    def weight_part(lhs, rhs, at, y):
        width = rhs.shape[1]
        part = dot(lhs[:, y * 256 : (y + 1) * 256], rhs, TN).astype(BF)
        g2[y, :, :, :, :, at : at + width] = part.reshape(4, 2, 2, 16, width)

    own_att = att_all[t]
    for y in range(4):
        weight_part(ml, own_att, 512, y)
        weight_part(nrm, dql[...], 0, y)
    pp[...] = dot(dql[...], wq[...], NT)

    first_sum(r0, ra0, first0)
    second0 = second_stage(r0, rb0, s0, q0)

    for half, total in enumerate(second_sum(r1, rb1, second1)):
        rows = slice(half * 16, half * 16 + 16)
        for n, ref in enumerate((gate_out, up_out, down_out)):
            ref[rows, :] = total[:, n * FF : (n + 1) * FF]

    key_grad, value_grad = second_sum(r0, rb0, second0)
    back, term = head_norm_back(kp[...], kg[...], rotate_back(key_grad))
    kvl[:, 0:128] = back.astype(BF)
    kvl[:, 128:256] = value_grad.astype(BF)
    key_gain_term = jnp.sum(term, 0, keepdims=True)

    ipb[...] = (pp[...] + dot(kvl[:, 0:128], wk[...], NT) + dot(kvl[:, 128:256], wv[...], NT)).astype(BF)
    in_c = [
        remote(ipb.at[rows_of(off(t, d))], xr.at[2, d - 1], xss.at[6, d - 1], xrs.at[6, d - 1], at_x(d))
        for d in order
    ]
    core2 = []
    for y in range(4):
        weight_part(nrm, kvl[...], 256, y)
        core2.append(core_stage(g2, r2, s2, q2, y))
    total = ipb[rows_of(t), :].astype(F32)
    for cp in in_c:
        cp.wait_recv()
    for d in range(3):
        total = total + xr[2, d].astype(F32)
    back, term = row_norm_back(x[rows_of(t), :].astype(F32), ng[...], total)
    xg_s[rows_of(t), :] = (mgr[...] + back).astype(BF)
    xg_c = [
        remote(xg_s.at[rows_of(t)], xg_s.at[rows_of(t)], xss.at[7, d - 1], xrs.at[7, d - 1], at_x(d))
        for d in order
    ]
    gv[0, 0:1, :] = jnp.sum(term, 0, keepdims=True)
    gv[0, 2:8, :] = jnp.zeros((6, 1024), F32)
    gv[0, 2:3, 0:128] = query_gain_term + pltpu.roll(query_gain_term, 64, 1)
    gv[0, 3:4, 0:128] = key_gain_term + pltpu.roll(key_gain_term, 64, 1)

    def gain_stage(n, peers):
        base = (0, 1, 4, 7)[n]
        return [
            remote(gv.at[n], gr.at[base + i], gss.at[base + i], grs.at[base + i], peer)
            for i, peer in enumerate(peers)
        ]

    def gain_sum(n, copies):
        base = (0, 1, 4, 7)[n]
        total = gv[n]
        for i, cp in enumerate(copies):
            cp.wait_recv()
            total = total + gr[base + i]
        return total

    gain_c = gain_stage(0, [at_k])
    for y in range(4):
        core_sum(g2, r2, y, core2[y])
    first2 = first_stage(r2, ra2, s2, q2)
    gv[1] = gain_sum(0, gain_c)
    gain_c = gain_stage(1, [at_x(d) for d in order])
    first_sum(r2, ra2, first2)
    second2 = second_stage(r2, rb2, s2, q2)
    gv[2] = gain_sum(1, gain_c)
    gain_c = gain_stage(2, [at_y(d) for d in order])
    for half, total in enumerate(second_sum(r2, rb2, second2)):
        attn_out[half * 16 : half * 16 + 16, :] = total
    gv[3] = gain_sum(2, gain_c)
    gain_c = gain_stage(3, [at_z(d) for d in order])
    for cp in mixed_c:
        cp.wait_recv()
    mixed_out[...] = mixed_s[...]
    for cp in xg_c:
        cp.wait_recv()
    xgrad_out[...] = xg_s[...]
    gains_out[...] = gain_sum(3, gain_c)
    for cp in sent:
        cp.wait_send()


def on_device(
    tokens, norm_gain, query_weight, key_weight, value_weight, query_gain, key_gain, out_weight,
    post_gain, gate_weight, up_weight, down_weight, cotangent,
):
    x = tokens.reshape(256, 1024)
    gy = cotangent.reshape(256, 1024)
    tables = [jnp.asarray(a) for a in rope_constants()]
    cr, sr, cb, sb = tables
    vm = pl.BlockSpec(memory_space=pltpu.VMEM)
    hbm = pl.BlockSpec(memory_space=pl.ANY)
    V = pltpu.VMEM
    sem = lambda *s: pltpu.SemaphoreType.DMA(s)
    scratch = [
        V((1024, FF), BF), V((1024, FF), BF), V((FF, 1024), BF), V((4, 256, 1024), BF),
        V((256, 1024), BF), V((2, 32, 256, 128), BF), V((256, 128), F32), V((2, 256, 128), F32),
        V((256, 128), F32), V((256, 128), F32), V((2, 512, 128), BF), V((2, 512, 128), BF),
        V((2, 128, 512), F32), V((2, 8, 512), F32), V((4, 256, 256), BF),
        V((256, 1024), F32), V((256, 1024), BF), V((256, FF), BF), V((256, FF), BF), V((256, FF), BF),
        V((256, 1024), F32), V((256, 1024), BF), V((256, 1024), BF), V((256, 1024), BF),
        V((3, 3, 64, 1024), BF),
        V((256, 1024), BF), V((64, 1024), F32), V((256, 1024), BF), V((256, 1024), BF),
        V((2, 512, 128), F32), V((256, 256), BF), V((256, 256), BF),
        V((4, 4, 2, 2, 16, GX), BF), V((4, 4, 2, 16, GX), BF), V((2, 3, 4, 16, GX), BF), V((2, 3, 16, GX), BF),
        V((4, 4, 2, 2, 256, 128), BF), V((4, 4, 2, 256, 128), BF), V((2, 3, 4, 256, 128), BF), V((2, 3, 256, 128), BF),
        V((4, 4, 2, 2, 16, G2X), BF), V((4, 4, 2, 16, G2X), BF), V((2, 3, 4, 16, G2X), BF), V((2, 3, 16, G2X), BF),
        V((4, 8, 1024), F32), V((10, 8, 1024), F32),
        sem(4), sem(2, 32), sem(2, 32), sem(8, 3), sem(8, 3),
        sem(16), sem(16), sem(16), sem(16), sem(16), sem(16), sem(10), sem(10),
    ]
    shape = jax.ShapeDtypeStruct
    mixed, xgrad, gains, gate, up, down, attn = pl.pallas_call(
        kernel,
        name="block",
        out_shape=[
            shape((256, 1024), BF), shape((256, 1024), BF), shape((8, 1024), F32),
            shape((32, FF), F32), shape((32, FF), F32), shape((32, FF), F32), shape((32, G2X), F32),
        ],
        in_specs=[vm] * 7 + [hbm] + [vm] + [hbm] * 3 + [vm] * 5,
        out_specs=[vm] * 7,
        scratch_shapes=scratch,
        compiler_params=pltpu.CompilerParams(
            collective_id=0, has_side_effects=True, vmem_limit_bytes=63 * 2**20
        ),
    )(
        x, norm_gain.reshape(1, 1024), query_weight, key_weight, value_weight,
        jnp.tile(query_gain, 2).reshape(1, 128), jnp.tile(key_gain, 2).reshape(1, 128),
        out_weight, post_gain.reshape(1, 1024), gate_weight, up_weight, down_weight, gy, cr, sr, cb, sb,
    )
    place = (2, 2, 1, 64, 1024)
    return (
        mixed.reshape(place), xgrad.reshape(place), gains[0], attn[:, 0:256], attn[:, 256:384],
        attn[:, 384:512], gains[2, 0:64], gains[3, 0:64], attn[:, 512:768].T, gains[1], gate, up, down.T,
    )


def solution(mesh):
    tok = P(None, None, "ctx", None, None)
    col = P(None, "tp")
    row = P("tp", None)
    return jax.shard_map(
        on_device,
        mesh=mesh,
        in_specs=(tok, P(), col, col, col, P(), P(), row, P(), col, col, row, tok),
        out_specs=(
            tok, tok, P(), P("ctx", "tp"), P("ctx", "tp"), P("ctx", "tp"), P(), P(), P("tp", "ctx"), P(),
            P("ctx", "tp"), P("ctx", "tp"), P("tp", "ctx"),
        ),
        check_vma=False,
    )
```

time: 1220 us -> 149 us (0.12)
  waiting for transfers between devices: 819 us -> 0 us
  blocking collectives: 138 us -> 0 us
  Pallas kernels: 0 us -> 134 us
  local copies, waits for them, and re-layouts: 97.9 us -> 13.7 us
  matrix products: 83.6 us -> 0 us
  other arithmetic: 58.8 us -> 0 us
  between operations: 15.5 us -> 0.68 us
    reduce_scatter x9 -> x0, waiting for transfers between devices: 629 us -> none  [the longest x1 80.9 us: on_device(): lax.psum_scatter(gate_weight_grad.astype(jnp.bfloat16), 'ctx', scatter_di...]
    psum x2 -> x0, blocking collectives: 138 us -> none  [the longest x1 127 us: on_device(): lax.psum((jnp.sum(norm_gain_term, 0), jnp.sum(post_gain_term, 0), query_g...]
    pallas_call x0 -> x1, Pallas kernels: none -> 134 us  [on_device(): pl.pallas_call(kernel, name='block', out_shape=[shape((256, 1024), BF), s...]
    psum x3 -> x0, waiting for transfers between devices: 128 us -> none  [the longest x1 46.8 us: on_device(): lax.psum(mlp_part.astype(jnp.bfloat16), 'tp').astype(jnp.float32)]
    dot_general x45 -> x0, matrix products: 83.6 us -> none  [the longest x4 10.6 us: on_device(): jnp.einsum('kgqs,qkgd->skd', probability.astype(jnp.bfloat16), grad_block...]
    all_gather x2 -> x0, waiting for transfers between devices: 61.1 us -> none  [the longest x1 33.5 us: on_device(): lax.all_gather(key_shard, 'ctx', axis=2, tiled=True)]
    another operation x6 -> x4, local copies, waits for them, and re-layouts: 29.1 us -> 2.5 us  [the longest x2 1.25 us: on_device(): jnp.tile(query_gain, 2).reshape(1, 128)]
    convert_element_type x18 -> x0, other arithmetic: 24 us -> none  [the longest x5 7.05 us: on_device(): query_weight_grad, key_weight_grad, value_weight_grad, gate_weight_grad,...]
  transfers between devices with their start and end apart: 14 -> 0, of which waited for: 14 -> 0; matrix products, arithmetic and copies ran while one was open for 10% -> 0% of each run, Pallas kernels for 0% -> 0%
where the time goes in v1:
time: 149 us; the launch traced here: 148 us
  Pallas kernels  134 us (90%)
  local copies, waits for them, and re-layouts  13.7 us (9%)
    pallas_call x1, Pallas kernels, on_device(): pl.pallas_call(kernel, name='block', out_shape=[shape((256, 1024), BF), s...  134 us
    unnamed x11, local copies, waits for them, and re-layouts  5.73 us

profile of v1, /device:TPU:0, one launch (start us, length us, event | category | flops | bytes accessed | tf_op | source)
XLA Modules:
  0.0 148.2 jit_solution(10229873390719857157)
XLA Ops:
  0.6 0.7 tile.4
  1.3 0.6 reshape_tile.6.qg
  1.9 0.7 tile.5
  2.6 0.6 reshape_tile.7.kg
  3.1 133.8 %block.1 = (bf16[256,1024]{1,0:T(8,128)(2,1)}, bf16[256,1024]{1,0:T(8,128)(2,1)}, f32[8,1024]{1,0:T(8,128)}, f32[32,1152]{1,0:T(8,128)}, f32[32,1152]{1,0:T(8,12...) custom-call(bf16[256,1024]{1,0:T(8,128)(2,1)} %bitcast.19, f32[1,1024]{1,0:T(1,128)} %bitcast.24, bf16[1024,256]{1,0:T(8,128)(2,1)} %wq.1, ...), custom_call_target="tpu_custom_call" | custom-call | tf_op jit(solution)/shard_map/block/pallas_call | solution.py:608
  137.0 0.0 copy-start.2
  137.0 0.0 copy-start.1
  137.0 0.0 copy-start
  137.0 1.5 slice_bitcast_fusion
  138.4 1.3 fusion
  139.8 1.4 fusion.1
  141.2 1.3 slice_bitcast_fusion.1
  142.5 1.9 %copy.37 = bf16[2,2,1,64,1024]{4,3,2,1,0:T(8,128)(2,1)} copy(bf16[2,2,1,64,1024]{4,3,2,1,0:T(8,128)(2,1)} %bitcast.22) | data formatting | bytes 1048576
  144.4 1.9 %copy.38 = bf16[2,2,1,64,1024]{4,3,2,1,0:T(8,128)(2,1)} copy(bf16[2,2,1,64,1024]{4,3,2,1,0:T(8,128)(2,1)} %bitcast.21) | data formatting | bytes 1048576
  146.2 0.0 copy-done.2
  146.2 0.7 copy.39
  146.9 0.0 copy-done.1
  146.9 0.7 copy.40
  147.6 0.0 copy-done
  147.6 0.7 copy.41
Async XLA Ops:
  137.0 9.3 %copy-start.2 = (f32[32,1152]{1,0:T(8,128)S(1)}, f32[32,1152]{1,0:T(8,128)}, u32[]{:S(2)}) copy-start(f32[32,1152]{1,0:T(8,128)} %get-tuple-element.71) | copy-start | bytes 442372
  137.0 9.9 %copy-start.1 = (f32[32,1152]{1,0:T(8,128)S(1)}, f32[32,1152]{1,0:T(8,128)}, u32[]{:S(2)}) copy-start(f32[32,1152]{1,0:T(8,128)} %get-tuple-element.72) | copy-start | bytes 442372
  137.0 10.6 %copy-start = (f32[32,1152]{1,0:T(8,128)S(1)}, f32[32,1152]{1,0:T(8,128)}, u32[]{:S(2)}) copy-start(f32[32,1152]{1,0:T(8,128)} %get-tuple-element.26) | copy-start | bytes 442372

commit v2 on v1

--- a/solution.py
+++ b/solution.py
@@ -13,8 +13,9 @@
 F32 = jnp.float32
 MESH = pl.DeviceIdType.MESH
 FF = 1152
-GX = 3 * FF
-G2X = 768
+G1X = 2 * FF
+G2X = 256
+G3X = FF + 512
 
 NN = (((1,), (0,)), ((), ()))
 NT = (((1,), (1,)), ((), ()))
@@ -94,11 +95,11 @@
 
 def kernel(
     x, ng, wq, wk, wv, qg, kg, wo_in, pg, wg_in, wu_in, wd_in, gy, cr, sr, cb, sb,
-    mixed_out, xgrad_out, gains_out, gate_out, up_out, down_out, attn_out,
+    mixed_out, xgrad_out, ng_out, wq_out, wk_out, wv_out, qg_out, kg_out, wo_out, pg_out, gate_out, up_out, down_out,
     wg, wu, wd, wo_all, nrm, kv_all, kp, qp, ct, st_, qbd, dobd, ot, stats, att_all,
     mid, post, hid, gg, ug, pp, ppb, mpb, ipb, xr, ml, mgr, mixed_s, xg_s, dq, dql, kvl,
-    g1, r1, ra1, rb1, dkv, r0, ra0, rb0, g2, r2, ra2, rb2, gv, gr,
-    loc, kss, krs, xss, xrs, s1, q1, s0, q0, s2, q2, gss, grs,
+    g1, r1, ra1, rb1, dkv, r0, ra0, rb0, g2, r2, ra2, rb2, g3, r3, ra3, rb3, gv, gr,
+    loc, kss, krs, xss, xrs, wss, wrs, s1, q1, s0, q0, s2, q2, s3, q3, bs0, bq0, gss, grs,
 ):
     c = lax.axis_index("ctx")
     t = lax.axis_index("tp")
@@ -138,10 +139,13 @@
 
     sent = []
 
-    def remote(src, dst, ssem, rsem, peer):
-        cp = pltpu.make_async_remote_copy(
+    def remote_copy(src, dst, ssem, rsem, peer):
+        return pltpu.make_async_remote_copy(
             src_ref=src, dst_ref=dst, send_sem=ssem, recv_sem=rsem, device_id=peer, device_id_type=MESH
         )
+
+    def remote(src, dst, ssem, rsem, peer):
+        cp = remote_copy(src, dst, ssem, rsem, peer)
         cp.start()
         sent.append(cp)
         return cp
@@ -165,9 +169,11 @@
     def rotate_back(u):
         return u * ct[...] - swap_halves(u) * st_[...]
 
+    key_gain = jnp.concatenate([kg[...], kg[...]], 1)
+    query_gain = jnp.concatenate([qg[...], qg[...]], 1)
     kproj = dot(nrm[...], wk[...])
     kp[...] = kproj
-    kv_all[0, c] = rotate(head_norm(kproj, kg[...])).astype(BF)
+    kv_all[0, c] = rotate(head_norm(kproj, key_gain)).astype(BF)
     kv_all[1, c] = dot(nrm[...], wv[...]).astype(BF)
 
     pl.semaphore_wait(barrier, 10)
@@ -196,14 +202,15 @@
         pass_on(1, 0, 0, "y", d)
 
     locals_[0].wait()
-    wo_c = [
-        remote(wo_all.at[t], wo_all.at[t], xss.at[0, d - 1], xrs.at[0, d - 1], at_x(d)) for d in order
-    ]
+    def out_half(n):
+        return wo_all.at[n, pl.ds(pl.multiple_of(ck * 128, 128), 128)]
+
+    wo_c = [remote(out_half(t), out_half(t), xss.at[0, d - 1], xrs.at[0, d - 1], at_x(d)) for d in order]
 
     for kv in range(2):
         proj = dot(nrm[...], wq[:, kv * 128 : (kv + 1) * 128])
         qp[kv] = proj
-        to_diagonal(rotate(head_norm(proj, qg[...])).astype(BF).astype(F32) * 0.125, kv, qbd)
+        to_diagonal(rotate(head_norm(proj, query_gain)).astype(BF).astype(F32) * 0.125, kv, qbd)
 
     for d in order:
         arrive[0, (d, 0, 0)].wait_recv()
@@ -220,6 +227,11 @@
             pass_on(0, a, b, "k", 1)
             arrive[1, (b, a, 0)].wait_recv()
             pass_on(1, b, a, "k", 1)
+    wo_k = []
+    for d, cp in zip(order, wo_c):
+        cp.wait_recv()
+        half = out_half(off(t, -d))
+        wo_k.append(remote(half, half, wss.at[d - 1], wrs.at[d - 1], at_k))
     for kind in range(2):
         for dy in range(4):
             for dz in range(4):
@@ -286,7 +298,7 @@
     ]
     for cp in locals_[1:]:
         cp.wait()
-    for cp in wo_c:
+    for cp in wo_k:
         cp.wait_recv()
     for cp in att_c:
         cp.wait_recv()
@@ -342,7 +354,6 @@
     ppb[...] = pp[...].astype(BF)
     post_c = scatter_x(ppb, 2)
     mpb[...] = dot(hid[...], wd[...]).astype(BF)
-    mlp_c = scatter_x(mpb, 3)
 
     def core_stage(g, r, ss, qs, y):
         return remote(g.at[y, :, sib], r.at[y], ss.at[y], qs.at[y], at_k)
@@ -395,12 +406,15 @@
             out.append(total)
         return out
 
+    def weight_part(g, lhs, rhs, at, y):
+        width = rhs.shape[1]
+        part = dot(lhs[:, y * 256 : (y + 1) * 256], rhs[...], TN).astype(BF)
+        g[y, :, :, :, :, at : at + width] = part.reshape(4, 2, 2, 16, width)
+
     core1 = []
     for y in range(4):
-        cols = slice(y * 256, (y + 1) * 256)
-        for n, (a, b) in enumerate(((post, gg), (post, ug), (gy, hid))):
-            part = dot(a[:, cols], b[...], TN).astype(BF)
-            g1[y, :, :, :, :, n * FF : (n + 1) * FF] = part.reshape(4, 2, 2, 16, FF)
+        weight_part(g1, post, gg, 0, y)
+        weight_part(g1, post, ug, FF, y)
         core1.append(core_stage(g1, r1, s1, q1, y))
 
     post_grad = collect_x(ppb, 2, post_c)
@@ -410,15 +424,15 @@
     ml_c = spread_x(ml, 4)
     gv[0, 1:2, :] = jnp.sum(post_gain_term, 0, keepdims=True)
 
-    mixed_s[rows_of(t), :] = (mid[rows_of(t), :] + collect_x(mpb, 3, mlp_c)).astype(BF)
-    mixed_c = spread_x(mixed_s, 5)
-
     for y in range(4):
         core_sum(g1, r1, y, core1[y])
     first1 = first_stage(r1, ra1, s1, q1)
 
+    for y in range(4):
+        weight_part(g3, gy, hid, 0, y)
     for cp in ml_c:
         cp.wait_recv()
+    mlp_c = scatter_x(mpb, 3)
 
     ag = dot(ml[...], wo_all[t], NT).astype(BF).astype(F32)
     for kv in range(2):
@@ -440,33 +454,69 @@
         dkv[j, :, :, 0, where, :] = dot(ds, q).astype(BF).reshape(4, 2, 64, 128)
         dq[s, at, :] += dot(ds, kc, TN)
 
-    def front_both(j, _):
-        for s in range(2):
-            back_step(j, s, 0, 0, lambda n: visible_front(n, 512))
+    def key_core(j):
+        return remote_copy(dkv.at[j, :, sib], r0.at[j], s0.at[j], q0.at[j], at_k)
+
+    def key_along_y(j):
+        d = lax.rem(j - cy + 4, 4)
+        peer = ((j * 4 + cz) * 2 + ck, t)
+        return remote_copy(r0.at[j, :, 0], ra0.at[0, d - 1], s0.at[3 + d], q0.at[3 + d], peer)
+
+    def key_along_z(j):
+        return [
+            remote_copy(r0.at[j, off(cz, d), 1], ra0.at[1, d - 1, j], bs0.at[d - 1, j], bq0.at[d - 1, j], at_z(d))
+            for d in order
+        ]
+
+    def key_step(j, _):
+        @pl.when(j < 4)
+        def _():
+            @pl.when(j <= cy)
+            def _():
+                for s in range(2):
+                    back_step(j, s, 0, 0, lambda n: visible_front(n, 512))
+
+            @pl.when(j > cy)
+            def _():
+                for s in range(2):
+                    back_step(j, s, 0, 256, None)
+
+            @pl.when(j >= cy)
+            def _():
+                for s in range(2):
+                    back_step(j, s, 1, 256, visible_back)
+
+            @pl.when(j < cy)
+            def _():
+                for s in range(2):
+                    for kind in range(2):
+                        dkv[j, :, :, kind, pl.ds((s * 2 + 1) * 64, 64), :] = jnp.zeros((4, 2, 64, 128), BF)
+
+            key_core(j).start()
+
+        @pl.when(j > 0)
+        def _():
+            core_sum(dkv, r0, j - 1, key_core(j - 1))
+
+            @pl.when(j - 1 != cy)
+            def _():
+                key_along_y(j - 1).start()
+
+            for cp in key_along_z(j - 1):
+                cp.start()
+
         return 0
 
-    def front_one(j, _):
-        for s in range(2):
-            back_step(j, s, 0, 256, None)
-        return 0
-
-    def behind_one(j, _):
-        for s in range(2):
-            back_step(j, s, 1, 256, visible_back)
-        return 0
-
-    def behind_none(j, _):
-        for s in range(2):
-            for kind in range(2):
-                dkv[j, :, :, kind, pl.ds((s * 2 + 1) * 64, 64), :] = jnp.zeros((4, 2, 64, 128), BF)
-        return 0
-
-    lax.fori_loop(0, own_chunk, behind_none, 0)
-    lax.fori_loop(0, own_chunk + 1, front_both, 0)
-    lax.fori_loop(own_chunk + 1, 4, front_one, 0)
-    lax.fori_loop(own_chunk, 4, behind_one, 0)
-
-    core0 = [core_stage(dkv, r0, s0, q0, y) for y in range(4)]
+    lax.fori_loop(0, 5, key_step, 0)
+    first0 = []
+    for y in range(4):
+        sent.append(key_core(y))
+        first0 += key_along_z(y)
+    for d in order:
+        first0.append(
+            remote_copy(r0.at[off(cy, d), :, 0], ra0.at[0, d - 1], s0.at[3 + d], q0.at[3 + d], at_y(d))
+        )
+    sent.extend(first0)
 
     query_gain_term = jnp.zeros((1, 128), F32)
     for kv in range(2):
@@ -474,38 +524,27 @@
             from_diagonal(dq[s, h * 256 : (h + 1) * 256, :], kv) for s in range(2) for h in range(2)
         ]
         grads = rotate_back(jnp.concatenate(parts, 0) * 0.125)
-        back, term = head_norm_back(qp[kv], qg[...], grads)
+        back, term = head_norm_back(qp[kv], query_gain, grads)
         dql[:, kv * 128 : (kv + 1) * 128] = back.astype(BF)
         query_gain_term = query_gain_term + jnp.sum(term, 0, keepdims=True)
 
-    for y in range(4):
-        core_sum(dkv, r0, y, core0[y])
-    first0 = first_stage(r0, ra0, s0, q0)
-
+    mixed_s[rows_of(t), :] = (mid[rows_of(t), :] + collect_x(mpb, 3, mlp_c)).astype(BF)
+    mixed_c = spread_x(mixed_s, 5)
+
+    first_sum(r0, ra0, first0)
+    second0 = second_stage(r0, rb0, s0, q0)
     first_sum(r1, ra1, first1)
     second1 = second_stage(r1, rb1, s1, q1)
 
-    def weight_part(lhs, rhs, at, y):
-        width = rhs.shape[1]
-        part = dot(lhs[:, y * 256 : (y + 1) * 256], rhs, TN).astype(BF)
-        g2[y, :, :, :, :, at : at + width] = part.reshape(4, 2, 2, 16, width)
-
-    own_att = att_all[t]
+    core3 = []
     for y in range(4):
-        weight_part(ml, own_att, 512, y)
-        weight_part(nrm, dql[...], 0, y)
+        weight_part(g3, ml, att_all.at[t], FF, y)
+        weight_part(g3, nrm, dql, FF + 256, y)
+        core3.append(core_stage(g3, r3, s3, q3, y))
     pp[...] = dot(dql[...], wq[...], NT)
 
-    first_sum(r0, ra0, first0)
-    second0 = second_stage(r0, rb0, s0, q0)
-
-    for half, total in enumerate(second_sum(r1, rb1, second1)):
-        rows = slice(half * 16, half * 16 + 16)
-        for n, ref in enumerate((gate_out, up_out, down_out)):
-            ref[rows, :] = total[:, n * FF : (n + 1) * FF]
-
     key_grad, value_grad = second_sum(r0, rb0, second0)
-    back, term = head_norm_back(kp[...], kg[...], rotate_back(key_grad))
+    back, term = head_norm_back(kp[...], key_gain, rotate_back(key_grad))
     kvl[:, 0:128] = back.astype(BF)
     kvl[:, 128:256] = value_grad.astype(BF)
     key_gain_term = jnp.sum(term, 0, keepdims=True)
@@ -515,64 +554,91 @@
         remote(ipb.at[rows_of(off(t, d))], xr.at[2, d - 1], xss.at[6, d - 1], xrs.at[6, d - 1], at_x(d))
         for d in order
     ]
-    core2 = []
     for y in range(4):
-        weight_part(nrm, kvl[...], 256, y)
-        core2.append(core_stage(g2, r2, s2, q2, y))
+        core_sum(g3, r3, y, core3[y])
+    first3 = first_stage(r3, ra3, s3, q3)
+    for y in range(4):
+        weight_part(g2, nrm, kvl, 0, y)
+    core2 = [core_stage(g2, r2, s2, q2, y) for y in range(4)]
+
+    for half, total in enumerate(second_sum(r1, rb1, second1)):
+        rows = slice(half * 16, half * 16 + 16)
+        gate_out[rows, :] = total[:, 0:FF]
+        up_out[rows, :] = total[:, FF : 2 * FF]
+    for y in range(4):
+        core_sum(g2, r2, y, core2[y])
+    first2 = first_stage(r2, ra2, s2, q2)
+
     total = ipb[rows_of(t), :].astype(F32)
     for cp in in_c:
         cp.wait_recv()
     for d in range(3):
         total = total + xr[2, d].astype(F32)
     back, term = row_norm_back(x[rows_of(t), :].astype(F32), ng[...], total)
+    gv[0, 0:1, :] = jnp.sum(term, 0, keepdims=True)
+    gv[0, 2:8, :] = jnp.zeros((6, 1024), F32)
+    gv[0, 2:3, 0:128] = query_gain_term + pltpu.roll(query_gain_term, 64, 1)
+    gv[0, 3:4, 0:128] = key_gain_term + pltpu.roll(key_gain_term, 64, 1)
+
+    bases = (0, 3, 4, 7)
+
+    def gain_stage(n, peers):
+        return [
+            remote(gv.at[n], gr.at[bases[n] + i], gss.at[bases[n] + i], grs.at[bases[n] + i], peer)
+            for i, peer in enumerate(peers)
+        ]
+
+    def gain_sum(n, copies):
+        total = gv[n]
+        for i, cp in enumerate(copies):
+            cp.wait_recv()
+            total = total + gr[bases[n] + i]
+        return total
+
+    gain_c = gain_stage(0, [at_x(d) for d in order])
     xg_s[rows_of(t), :] = (mgr[...] + back).astype(BF)
     xg_c = [
         remote(xg_s.at[rows_of(t)], xg_s.at[rows_of(t)], xss.at[7, d - 1], xrs.at[7, d - 1], at_x(d))
         for d in order
     ]
-    gv[0, 0:1, :] = jnp.sum(term, 0, keepdims=True)
-    gv[0, 2:8, :] = jnp.zeros((6, 1024), F32)
-    gv[0, 2:3, 0:128] = query_gain_term + pltpu.roll(query_gain_term, 64, 1)
-    gv[0, 3:4, 0:128] = key_gain_term + pltpu.roll(key_gain_term, 64, 1)
-
-    def gain_stage(n, peers):
-        base = (0, 1, 4, 7)[n]
-        return [
-            remote(gv.at[n], gr.at[base + i], gss.at[base + i], grs.at[base + i], peer)
-            for i, peer in enumerate(peers)
-        ]
-
-    def gain_sum(n, copies):
-        base = (0, 1, 4, 7)[n]
-        total = gv[n]
-        for i, cp in enumerate(copies):
-            cp.wait_recv()
-            total = total + gr[base + i]
-        return total
-
-    gain_c = gain_stage(0, [at_k])
-    for y in range(4):
-        core_sum(g2, r2, y, core2[y])
-    first2 = first_stage(r2, ra2, s2, q2)
     gv[1] = gain_sum(0, gain_c)
-    gain_c = gain_stage(1, [at_x(d) for d in order])
+    gain_c = gain_stage(1, [at_k])
+    first_sum(r3, ra3, first3)
+    second3 = second_stage(r3, rb3, s3, q3)
+    gv[2] = gain_sum(1, gain_c)
+    gain_c = gain_stage(2, [at_y(d) for d in order])
     first_sum(r2, ra2, first2)
     second2 = second_stage(r2, rb2, s2, q2)
-    gv[2] = gain_sum(1, gain_c)
-    gain_c = gain_stage(2, [at_y(d) for d in order])
-    for half, total in enumerate(second_sum(r2, rb2, second2)):
-        attn_out[half * 16 : half * 16 + 16, :] = total
-    gv[3] = gain_sum(2, gain_c)
-    gain_c = gain_stage(3, [at_z(d) for d in order])
     for cp in mixed_c:
         cp.wait_recv()
     mixed_out[...] = mixed_s[...]
+    gv[3] = gain_sum(2, gain_c)
+    gain_c = gain_stage(3, [at_z(d) for d in order])
+    for half, total in enumerate(second_sum(r3, rb3, second3)):
+        rows = slice(half * 16, half * 16 + 16)
+        down_out[rows, :] = total[:, 0:FF]
+        wo_out[rows, :] = total[:, FF : FF + 256]
+        wq_out[rows, :] = total[:, FF + 256 : FF + 512]
+    for half, total in enumerate(second_sum(r2, rb2, second2)):
+        rows = slice(half * 16, half * 16 + 16)
+        wk_out[rows, :] = total[:, 0:128]
+        wv_out[rows, :] = total[:, 128:256]
     for cp in xg_c:
         cp.wait_recv()
     xgrad_out[...] = xg_s[...]
-    gains_out[...] = gain_sum(3, gain_c)
+    gains = gain_sum(3, gain_c)
+    ng_out[...] = gains[0:1, :]
+    pg_out[...] = gains[1:2, :]
+    qg_out[...] = gains[2:3, 0:64]
+    kg_out[...] = gains[3:4, 0:64]
     for cp in sent:
         cp.wait_send()
+
+
+def hand_out(*refs):
+    count = len(refs) // 2
+    for source, target in zip(refs[:count], refs[count:]):
+        target[...] = source[...]
 
 
 def on_device(
@@ -587,6 +653,10 @@
     hbm = pl.BlockSpec(memory_space=pl.ANY)
     V = pltpu.VMEM
     sem = lambda *s: pltpu.SemaphoreType.DMA(s)
+
+    def ring(rows, width):
+        return [V(lead + (rows, width), BF) for lead in ((4, 4, 2, 2), (4, 4, 2), (2, 3, 4), (2, 3))]
+
     scratch = [
         V((1024, FF), BF), V((1024, FF), BF), V((FF, 1024), BF), V((4, 256, 1024), BF),
         V((256, 1024), BF), V((2, 32, 256, 128), BF), V((256, 128), F32), V((2, 256, 128), F32),
@@ -597,36 +667,48 @@
         V((3, 3, 64, 1024), BF),
         V((256, 1024), BF), V((64, 1024), F32), V((256, 1024), BF), V((256, 1024), BF),
         V((2, 512, 128), F32), V((256, 256), BF), V((256, 256), BF),
-        V((4, 4, 2, 2, 16, GX), BF), V((4, 4, 2, 16, GX), BF), V((2, 3, 4, 16, GX), BF), V((2, 3, 16, GX), BF),
-        V((4, 4, 2, 2, 256, 128), BF), V((4, 4, 2, 256, 128), BF), V((2, 3, 4, 256, 128), BF), V((2, 3, 256, 128), BF),
-        V((4, 4, 2, 2, 16, G2X), BF), V((4, 4, 2, 16, G2X), BF), V((2, 3, 4, 16, G2X), BF), V((2, 3, 16, G2X), BF),
+        *ring(16, G1X),
+        *ring(256, 128),
+        *ring(16, G2X),
+        *ring(16, G3X),
         V((4, 8, 1024), F32), V((10, 8, 1024), F32),
-        sem(4), sem(2, 32), sem(2, 32), sem(8, 3), sem(8, 3),
-        sem(16), sem(16), sem(16), sem(16), sem(16), sem(16), sem(10), sem(10),
+        sem(4), sem(2, 32), sem(2, 32), sem(8, 3), sem(8, 3), sem(3), sem(3),
+        *[sem(16)] * 8, sem(3, 4), sem(3, 4), sem(10), sem(10),
     ]
     shape = jax.ShapeDtypeStruct
-    mixed, xgrad, gains, gate, up, down, attn = pl.pallas_call(
+    outs = [
+        shape((256, 1024), BF), shape((256, 1024), BF), shape((1, 1024), F32),
+        shape((32, 256), F32), shape((32, 128), F32), shape((32, 128), F32),
+        shape((1, 64), F32), shape((1, 64), F32), shape((32, 256), F32), shape((1, 1024), F32),
+        shape((32, FF), F32), shape((32, FF), F32), shape((32, FF), F32),
+    ]
+    results = pl.pallas_call(
         kernel,
         name="block",
-        out_shape=[
-            shape((256, 1024), BF), shape((256, 1024), BF), shape((8, 1024), F32),
-            shape((32, FF), F32), shape((32, FF), F32), shape((32, FF), F32), shape((32, G2X), F32),
-        ],
+        out_shape=outs,
         in_specs=[vm] * 7 + [hbm] + [vm] + [hbm] * 3 + [vm] * 5,
-        out_specs=[vm] * 7,
+        out_specs=[vm] * 13,
         scratch_shapes=scratch,
         compiler_params=pltpu.CompilerParams(
             collective_id=0, has_side_effects=True, vmem_limit_bytes=63 * 2**20
         ),
     )(
         x, norm_gain.reshape(1, 1024), query_weight, key_weight, value_weight,
-        jnp.tile(query_gain, 2).reshape(1, 128), jnp.tile(key_gain, 2).reshape(1, 128),
+        query_gain.reshape(1, 64), key_gain.reshape(1, 64),
         out_weight, post_gain.reshape(1, 1024), gate_weight, up_weight, down_weight, gy, cr, sr, cb, sb,
     )
+    results = pl.pallas_call(
+        hand_out,
+        name="hand_out",
+        out_shape=outs,
+        in_specs=[vm] * 13,
+        out_specs=[vm] * 13,
+    )(*results)
+    mixed, xgrad, ng, wq, wk, wv, qg, kg, wo, pg, gate, up, down = results
     place = (2, 2, 1, 64, 1024)
     return (
-        mixed.reshape(place), xgrad.reshape(place), gains[0], attn[:, 0:256], attn[:, 256:384],
-        attn[:, 384:512], gains[2, 0:64], gains[3, 0:64], attn[:, 512:768].T, gains[1], gate, up, down.T,
+        mixed.reshape(place), xgrad.reshape(place), ng.reshape(1024), wq, wk, wv, qg.reshape(64), kg.reshape(64),
+        wo.T, pg.reshape(1024), gate, up, down.T,
     )
 
 

time: 149 us -> 129 us (0.87)
  local copies, waits for them, and re-layouts: 13.7 us -> 0 us
  Pallas kernels: 134 us -> 128 us
    pallas_call x1 -> x2, Pallas kernels: 134 us -> 128 us  [the longest x1 125 us: on_device(): pl.pallas_call(kernel, name='block', out_shape=outs, in_specs=[vm] * 7 +...]
    unnamed x11 -> x0, local copies, waits for them, and re-layouts: 5.73 us -> none
    slice x2 -> x0, local copies, waits for them, and re-layouts: 2.78 us -> none  [the longest x1 1.44 us: on_device(): gains[1]]
    another operation x4 -> x0, local copies, waits for them, and re-layouts: 2.5 us -> none  [the longest x2 1.25 us: on_device(): jnp.tile(query_gain, 2).reshape(1, 128)]
where the time goes in v2:
time: 129 us; the launch traced here: 128 us
  Pallas kernels  128 us (99%)
    pallas_call x1, Pallas kernels, on_device(): pl.pallas_call(kernel, name='block', out_shape=outs, in_specs=[vm] * 7 +...  125 us

profile of v2, /device:TPU:0, one launch (start us, length us, event | category | flops | bytes accessed | tf_op | source)
XLA Modules:
  0.0 128.5 jit_solution(16273960701542177188)
XLA Ops:
  0.6 125.2 %block.1 = (bf16[256,1024]{1,0:T(8,128)(2,1)}, bf16[256,1024]{1,0:T(8,128)(2,1)}, f32[1,1024]{1,0:T(1,128)}, f32[32,256]{1,0:T(8,128)}, f32[32,128]{1,0:T(8,128)...) custom-call(bf16[256,1024]{1,0:T(8,128)(2,1)} %bitcast.18, ...), custom_call_target="tpu_custom_call" | custom-call | tf_op jit(solution)/shard_map/block/pallas_call | solution.py:685
  125.8 2.6 %hand_out.1 = (bf16[256,1024]{1,0:T(8,128)(2,1)}, bf16[256,1024]{1,0:T(8,128)(2,1)}, f32[1,1024]{1,0:T(1,128)}, f32[32,256]{1,0:T(8,128)}, f32[32,128]{1,0:T(8,1...) custom-call(bf16[256,1024]{1,0:T(8,128)(2,1)} %get-tuple-element.39., ...), custom_call_target="tpu_custom_call" | custom-call | tf_op jit(solution)/shard_map/hand_out/pallas_call | solution.py:700

commit v3 on v2

--- a/solution.py
+++ b/solution.py
@@ -96,7 +96,7 @@
 def kernel(
     x, ng, wq, wk, wv, qg, kg, wo_in, pg, wg_in, wu_in, wd_in, gy, cr, sr, cb, sb,
     mixed_out, xgrad_out, ng_out, wq_out, wk_out, wv_out, qg_out, kg_out, wo_out, pg_out, gate_out, up_out, down_out,
-    wg, wu, wd, wo_all, nrm, kv_all, kp, qp, ct, st_, qbd, dobd, ot, stats, att_all,
+    wg, wu, wd, wo_all, nrm, kv_all, kp, qp, ct, st_, qbd, dobd, ot, sums, stats, att_all,
     mid, post, hid, gg, ug, pp, ppb, mpb, ipb, xr, ml, mgr, mixed_s, xg_s, dq, dql, kvl,
     g1, r1, ra1, rb1, dkv, r0, ra0, rb0, g2, r2, ra2, rb2, g3, r3, ra3, rb3, gv, gr,
     loc, kss, krs, xss, xrs, wss, wrs, s1, q1, s0, q0, s2, q2, s3, q3, bs0, bq0, gss, grs,
@@ -205,97 +205,110 @@
     def out_half(n):
         return wo_all.at[n, pl.ds(pl.multiple_of(ck * 128, 128), 128)]
 
-    wo_c = [remote(out_half(t), out_half(t), xss.at[0, d - 1], xrs.at[0, d - 1], at_x(d)) for d in order]
+    wo_c = [remote(out_half(t), out_half(t), xss.at[8, d - 1], xrs.at[8, d - 1], at_x(d)) for d in order]
 
     for kv in range(2):
         proj = dot(nrm[...], wq[:, kv * 128 : (kv + 1) * 128])
         qp[kv] = proj
         to_diagonal(rotate(head_norm(proj, query_gain)).astype(BF).astype(F32) * 0.125, kv, qbd)
 
+    def seq_rows(s, kh):
+        return pl.ds(pl.multiple_of((s * 2 + kh) * 64, 64), 64)
+
+    def chunk(kind, j, s, kh):
+        return kv_all[kind, pl.ds(j * 8, 8), seq_rows(s, kh), :].reshape(512, 128)
+
+    def visible_front(width):
+        keys = lax.broadcasted_iota(jnp.int32, (512, width), 0)
+        lane = lax.broadcasted_iota(jnp.int32, (512, width), 1)
+        return (keys <= lax.rem(c, 8) * 64 + lane % 64) | (lane >= 256)
+
+    def visible_back():
+        keys = lax.broadcasted_iota(jnp.int32, (512, 256), 0)
+        lane = lax.broadcasted_iota(jnp.int32, (512, 256), 1)
+        return keys % 64 - 64 * (keys // 64) <= lane % 64 - 64 * lax.rem(c, 8)
+
+    def tile(s, j, kh, h, seen):
+        p = jnp.exp(dot(chunk(0, j, s, kh), qbd[s, pl.ds(pl.multiple_of(h * 256, 256), 256), :], NT))
+        if seen is not None:
+            p = jnp.where(seen, p, 0.0)
+        sums[s, h, 0:1, :] += jnp.sum(p, 0, keepdims=True)
+        ot[s, h] += dot(chunk(1, j, s, kh), p.astype(BF), TN)
+
+    def attend(s, dy):
+        j = off(cy, -dy)
+        if dy == 0:
+            tile(s, j, 0, 0, visible_front(256))
+            tile(s, j, 0, 1, None)
+            tile(s, j, 1, 1, visible_back())
+        else:
+            later = jnp.where(j > cy, 1, 0)
+            tile(s, j, 0, 1, None)
+            tile(s, j, later, later, None)
+
+    def await_sibling(dy):
+        for kind in range(2):
+            for dz in range(4):
+                arrive[kind, (dy, dz, 1)].wait_recv()
+
+    ot[...] = jnp.zeros_like(ot)
+    sums[...] = jnp.zeros_like(sums)
     for d in order:
         arrive[0, (d, 0, 0)].wait_recv()
         for e in order:
             pass_on(0, d, 0, "z", e)
         pass_on(0, d, 0, "k", 1)
+    for d in order:
         arrive[1, (0, d, 0)].wait_recv()
+        pass_on(1, 0, d, "k", 1)
+    for d in order:
         for e in order:
-            pass_on(1, 0, d, "y", e)
-        pass_on(1, 0, d, "k", 1)
-    for a in (0, 1, 3, 2):
-        for b in order:
-            arrive[0, (a, b, 0)].wait_recv()
-            pass_on(0, a, b, "k", 1)
-            arrive[1, (b, a, 0)].wait_recv()
-            pass_on(1, b, a, "k", 1)
+            pass_on(1, 0, e, "y", d)
+
+    def pass_row(dy):
+        for e in order:
+            arrive[0, (dy, e, 0)].wait_recv()
+            pass_on(0, dy, e, "k", 1)
+        if dy > 0:
+            for e in (0,) + order:
+                arrive[1, (dy, e, 0)].wait_recv()
+                pass_on(1, dy, e, "k", 1)
+
+    pass_row(0)
+    await_sibling(0)
+    for s in range(2):
+        attend(s, 0)
+    pass_row(1)
+    pass_row(3)
+    await_sibling(1)
+    for s in range(2):
+        attend(s, 1)
     wo_k = []
     for d, cp in zip(order, wo_c):
         cp.wait_recv()
         half = out_half(off(t, -d))
         wo_k.append(remote(half, half, wss.at[d - 1], wrs.at[d - 1], at_k))
-    for kind in range(2):
-        for dy in range(4):
-            for dz in range(4):
-                arrive[kind, (dy, dz, 1)].wait_recv()
-
-    own_chunk = cy
-
-    def chunk(kind, j, s, kh):
-        return kv_all[kind, pl.ds(j * 8, 8), pl.ds((s * 2 + kh) * 64, 64), :].reshape(512, 128)
-
-    def visible_front(j, width):
-        keys = j * 512 + lax.broadcasted_iota(jnp.int32, (512, width), 0)
-        lane = lax.broadcasted_iota(jnp.int32, (512, width), 1)
-        return (keys <= c * 64 + lane % 64) | (lane >= 256)
-
-    def visible_back(j):
-        keys = lax.broadcasted_iota(jnp.int32, (512, 256), 0)
-        lane = lax.broadcasted_iota(jnp.int32, (512, 256), 1)
-        return keys % 64 - 64 * (j * 8 + keys // 64) <= lane % 64 - 64 * c
-
-    def forward_step(j, carry, h, kh, mask):
-        out = []
-        seen = mask(j) if mask is not None else None
-        for s in range(2):
-            m, l = carry[s]
-            scores = dot(chunk(0, j, s, kh), qbd[s, h * 256 : (h + 1) * 256, :], NT)
-            if seen is not None:
-                scores = jnp.where(seen, scores, -1e30)
-            new = jnp.maximum(m, jnp.max(scores, 0, keepdims=True))
-            p = jnp.exp(scores - new)
-            scale = jnp.exp(m - new)
-            l = l * scale + jnp.sum(p, 0, keepdims=True)
-            ot[s, :, h * 256 : (h + 1) * 256] = ot[s, :, h * 256 : (h + 1) * 256] * scale + dot(
-                chunk(1, j, s, kh), p.astype(BF), TN
-            )
-            out.append((new, l))
-        return tuple(out)
-
-    ot[...] = jnp.zeros_like(ot)
-    start = tuple((jnp.full((1, 256), -1e30, F32), jnp.zeros((1, 256), F32)) for _ in range(2))
-    totals = [None, None]
-    totals[0] = lax.fori_loop(
-        0, own_chunk + 1, lambda j, v: forward_step(j, v, 0, 0, lambda n: visible_front(n, 256)), start
-    )
-    run = lax.fori_loop(0, 4, lambda j, v: forward_step(j, v, 1, 0, None), start)
-    totals[1] = lax.fori_loop(
-        own_chunk, 4, lambda j, v: forward_step(j, v, 1, 1, visible_back), run
-    )
+    pass_row(2)
+    await_sibling(3)
     for s in range(2):
+        attend(s, 3)
+    await_sibling(2)
+    att_c = []
+    for s in range(2):
+        attend(s, 2)
         for h in range(2):
-            m, l = totals[h][s]
-            cols = slice(h * 256, (h + 1) * 256)
-            o = ot[s, :, cols] / l
-            ot[s, :, cols] = o
-            stats[s, 0:1, cols] = m + jnp.log(l)
+            l = sums[s, h, 0:1, :]
+            o = ot[s, h] / l
+            ot[s, h] = o
+            stats[s, 0:1, h * 256 : (h + 1) * 256] = jnp.log(l)
             rows = o.T
             for kv in range(2):
                 att_all[t, pl.ds((s * 2 + h) * 64, 64), kv * 128 : (kv + 1) * 128] = from_diagonal(
                     rows, kv
                 ).astype(BF)
-
-    att_c = [
-        remote(att_all.at[t], att_all.at[t], xss.at[1, d - 1], xrs.at[1, d - 1], at_x(d)) for d in order
-    ]
+        part = att_all.at[t, pl.ds(s * 128, 128)]
+        att_c += [remote(part, part, xss.at[s, d - 1], xrs.at[s, d - 1], at_x(d)) for d in order]
+
     for cp in locals_[1:]:
         cp.wait()
     for cp in wo_k:
@@ -438,16 +451,18 @@
     for kv in range(2):
         to_diagonal(ag[:, kv * 128 : (kv + 1) * 128], kv, dobd)
     for s in range(2):
-        stats[s, 1:2, :] = jnp.sum(dobd[s].astype(F32).T * ot[s], 0, keepdims=True)
+        for h in range(2):
+            at = slice(h * 256, (h + 1) * 256)
+            stats[s, 1:2, at] = jnp.sum(dobd[s, at, :].astype(F32).T * ot[s, h], 0, keepdims=True)
     dq[...] = jnp.zeros_like(dq)
 
-    def back_step(j, s, kh, first, mask):
+    def back_step(j, s, kh, first, seen):
         at = slice(first, 512)
         kc, vc = chunk(0, j, s, kh), chunk(1, j, s, kh)
         q, do = qbd[s, at, :], dobd[s, at, :]
         p = jnp.exp(dot(kc, q, NT) - stats[s, 0:1, at])
-        if mask is not None:
-            p = jnp.where(mask(j), p, 0.0)
+        if seen is not None:
+            p = jnp.where(seen, p, 0.0)
         ds = (p * (dot(vc, do, NT) - stats[s, 1:2, at])).astype(BF)
         where = pl.ds((s * 2 + kh) * 64, 64)
         dkv[j, :, :, 1, where, :] = dot(p.astype(BF), do).astype(BF).reshape(4, 2, 64, 128)
@@ -468,41 +483,42 @@
             for d in order
         ]
 
-    def key_step(j, _):
-        @pl.when(j < 4)
+    def key_step(n, _):
+        j = off(cy, n + 1)
+
+        @pl.when(n < 4)
         def _():
-            @pl.when(j <= cy)
+            @pl.when(j < cy)
             def _():
                 for s in range(2):
-                    back_step(j, s, 0, 0, lambda n: visible_front(n, 512))
+                    back_step(j, s, 0, 0, None)
+                    for kind in range(2):
+                        dkv[j, :, :, kind, pl.ds((s * 2 + 1) * 64, 64), :] = jnp.zeros((4, 2, 64, 128), BF)
 
             @pl.when(j > cy)
             def _():
                 for s in range(2):
                     back_step(j, s, 0, 256, None)
-
-            @pl.when(j >= cy)
+                    back_step(j, s, 1, 256, None)
+
+            @pl.when(j == cy)
             def _():
                 for s in range(2):
-                    back_step(j, s, 1, 256, visible_back)
-
-            @pl.when(j < cy)
+                    back_step(j, s, 0, 0, visible_front(512))
+                    back_step(j, s, 1, 256, visible_back())
+
+            key_core(j).start()
+
+        @pl.when(n > 0)
+        def _():
+            done = off(cy, n)
+            core_sum(dkv, r0, done, key_core(done))
+
+            @pl.when(n < 4)
             def _():
-                for s in range(2):
-                    for kind in range(2):
-                        dkv[j, :, :, kind, pl.ds((s * 2 + 1) * 64, 64), :] = jnp.zeros((4, 2, 64, 128), BF)
-
-            key_core(j).start()
-
-        @pl.when(j > 0)
-        def _():
-            core_sum(dkv, r0, j - 1, key_core(j - 1))
-
-            @pl.when(j - 1 != cy)
-            def _():
-                key_along_y(j - 1).start()
-
-            for cp in key_along_z(j - 1):
+                key_along_y(done).start()
+
+            for cp in key_along_z(done):
                 cp.start()
 
         return 0
@@ -661,7 +677,7 @@
         V((1024, FF), BF), V((1024, FF), BF), V((FF, 1024), BF), V((4, 256, 1024), BF),
         V((256, 1024), BF), V((2, 32, 256, 128), BF), V((256, 128), F32), V((2, 256, 128), F32),
         V((256, 128), F32), V((256, 128), F32), V((2, 512, 128), BF), V((2, 512, 128), BF),
-        V((2, 128, 512), F32), V((2, 8, 512), F32), V((4, 256, 256), BF),
+        V((2, 2, 128, 256), F32), V((2, 2, 8, 256), F32), V((2, 8, 512), F32), V((4, 256, 256), BF),
         V((256, 1024), F32), V((256, 1024), BF), V((256, FF), BF), V((256, FF), BF), V((256, FF), BF),
         V((256, 1024), F32), V((256, 1024), BF), V((256, 1024), BF), V((256, 1024), BF),
         V((3, 3, 64, 1024), BF),
@@ -672,7 +688,7 @@
         *ring(16, G2X),
         *ring(16, G3X),
         V((4, 8, 1024), F32), V((10, 8, 1024), F32),
-        sem(4), sem(2, 32), sem(2, 32), sem(8, 3), sem(8, 3), sem(3), sem(3),
+        sem(4), sem(2, 32), sem(2, 32), sem(9, 3), sem(9, 3), sem(3), sem(3),
         *[sem(16)] * 8, sem(3, 4), sem(3, 4), sem(10), sem(10),
     ]
     shape = jax.ShapeDtypeStruct

time: 129 us -> 116 us (0.90)
  Pallas kernels: 128 us -> 115 us
    pallas_call x1, Pallas kernels: 125 us -> 113 us  [on_device(): pl.pallas_call(kernel, name='block', out_shape=outs, in_specs=[vm] * 7 +...]
where the time goes in v3:
time: 116 us
  Pallas kernels  115 us (99%)
    pallas_call x1, Pallas kernels, on_device(): pl.pallas_call(kernel, name='block', out_shape=outs, in_specs=[vm] * 7 +...  113 us
    pallas_call x1, Pallas kernels, on_device(): pl.pallas_call(hand_out, name='hand_out', out_shape=outs, in_specs=[vm] *...  2.58 us

profile of v3, /device:TPU:0, one launch (start us, length us, event | category | flops | bytes accessed | tf_op | source)
XLA Modules:
  0.0 116.2 jit_solution(15274231626114382111)
XLA Ops:
  0.6 112.8 %block.1 = (bf16[256,1024]{1,0:T(8,128)(2,1)}, bf16[256,1024]{1,0:T(8,128)(2,1)}, f32[1,1024]{1,0:T(1,128)}, f32[32,256]{1,0:T(8,128)}, f32[32,128]{1,0:T(8,128)...) custom-call(bf16[256,1024]{1,0:T(8,128)(2,1)} %bitcast.18, ...), custom_call_target="tpu_custom_call" | custom-call | tf_op jit(solution)/shard_map/block/pallas_call | solution.py:701
  113.5 2.6 %hand_out.1 = (bf16[256,1024]{1,0:T(8,128)(2,1)}, bf16[256,1024]{1,0:T(8,128)(2,1)}, f32[1,1024]{1,0:T(1,128)}, f32[32,256]{1,0:T(8,128)}, f32[32,128]{1,0:T(8,1...) custom-call(bf16[256,1024]{1,0:T(8,128)(2,1)} %get-tuple-element.39., ...), custom_call_target="tpu_custom_call" | custom-call | tf_op jit(solution)/shard_map/hand_out/pallas_call | solution.py:716

commit v4 on v3

--- a/solution.py
+++ b/solution.py
@@ -94,12 +94,12 @@
 
 
 def kernel(
-    x, ng, wq, wk, wv, qg, kg, wo_in, pg, wg_in, wu_in, wd_in, gy, cr, sr, cb, sb,
+    x, ng, wq_in, wk, wv, qg, kg, wo_in, pg, wg_in, wu_in, wd_in, gy_in, cr, sr, cb, sb,
     mixed_out, xgrad_out, ng_out, wq_out, wk_out, wv_out, qg_out, kg_out, wo_out, pg_out, gate_out, up_out, down_out,
-    wg, wu, wd, wo_all, nrm, kv_all, kp, qp, ct, st_, qbd, dobd, ot, sums, stats, att_all,
+    wg, wu, wd, wq, gy, wo_all, nrm, kv_all, kp, qp, ct, st_, qbd, dobd, ot, sums, stats, att_all,
     mid, post, hid, gg, ug, pp, ppb, mpb, ipb, xr, ml, mgr, mixed_s, xg_s, dq, dql, kvl,
     g1, r1, ra1, rb1, dkv, r0, ra0, rb0, g2, r2, ra2, rb2, g3, r3, ra3, rb3, gv, gr,
-    loc, kss, krs, xss, xrs, wss, wrs, s1, q1, s0, q0, s2, q2, s3, q3, bs0, bq0, gss, grs,
+    loc, kss, krs, xss, xrs, yss, yrs, wss, wrs, s1, q1, s0, q0, s2, q2, s3, q3, bs0, bq0, gss, grs,
 ):
     c = lax.axis_index("ctx")
     t = lax.axis_index("tp")
@@ -120,18 +120,22 @@
     def at_x(d):
         return (c, off(t, d))
 
-    at_k = ((cy * 4 + cz) * 2 + sib, t)
+    def at_ky(d):
+        return ((off(cy, d) * 4 + cz) * 2 + sib, t)
+
+    at_k = at_ky(0)
     order = (1, 3, 2)
 
     barrier = pltpu.get_barrier_semaphore()
     for d in order:
         for peer in (at_x(d), at_y(d), at_z(d)):
             pl.semaphore_signal(barrier, inc=1, device_id=peer, device_id_type=MESH)
-    pl.semaphore_signal(barrier, inc=1, device_id=at_k, device_id_type=MESH)
+    for d in range(4):
+        pl.semaphore_signal(barrier, inc=1, device_id=at_ky(d), device_id_type=MESH)
 
     locals_ = []
     for n, (src, dst) in enumerate(
-        ((wo_in, wo_all.at[t]), (wg_in, wg), (wu_in, wu), (wd_in, wd))
+        ((wo_in, wo_all.at[t]), (wq_in, wq), (wg_in, wg), (wu_in, wu), (wd_in, wd), (gy_in, gy))
     ):
         cp = pltpu.make_async_copy(src, dst, loc.at[n])
         cp.start()
@@ -176,7 +180,7 @@
     kv_all[0, c] = rotate(head_norm(kproj, key_gain)).astype(BF)
     kv_all[1, c] = dot(nrm[...], wv[...]).astype(BF)
 
-    pl.semaphore_wait(barrier, 10)
+    pl.semaphore_wait(barrier, 13)
 
     arrive = {}
 
@@ -207,6 +211,7 @@
 
     wo_c = [remote(out_half(t), out_half(t), xss.at[8, d - 1], xrs.at[8, d - 1], at_x(d)) for d in order]
 
+    locals_[1].wait()
     for kv in range(2):
         proj = dot(nrm[...], wq[:, kv * 128 : (kv + 1) * 128])
         qp[kv] = proj
@@ -307,9 +312,9 @@
                     rows, kv
                 ).astype(BF)
         part = att_all.at[t, pl.ds(s * 128, 128)]
-        att_c += [remote(part, part, xss.at[s, d - 1], xrs.at[s, d - 1], at_x(d)) for d in order]
-
-    for cp in locals_[1:]:
+        att_c += [remote(part, part, xss.at[6 + s, d - 1], xrs.at[6 + s, d - 1], at_x(d)) for d in order]
+
+    for cp in locals_[2:]:
         cp.wait()
     for cp in wo_k:
         cp.wait_recv()
@@ -321,8 +326,6 @@
         branch = branch + dot(att_all[n], wo_all[n])
     mid[...] = x[...].astype(F32) + branch
     post[...] = (mid[...] * row_inverse(mid[...]) * pg[...]).astype(BF)
-
-    pp[...] = jnp.zeros_like(pp)
 
     def mlp_step(n, _):
         cols = pl.ds(pl.multiple_of(n * 384, 128), 384)
@@ -332,11 +335,8 @@
         sg = 1.0 / (1.0 + jnp.exp(-g))
         silu = g * sg
         hid[:, cols] = (silu * u).astype(BF)
-        a = (hgrad * u * sg * (1.0 + g * (1.0 - sg))).astype(BF)
-        b = (hgrad * silu).astype(BF)
-        gg[:, cols] = a
-        ug[:, cols] = b
-        pp[...] += dot(a, wg[:, cols], NT) + dot(b, wu[:, cols], NT)
+        gg[:, cols] = (hgrad * u * sg * (1.0 + g * (1.0 - sg))).astype(BF)
+        ug[:, cols] = (hgrad * silu).astype(BF)
         return 0
 
     lax.fori_loop(0, 3, mlp_step, 0)
@@ -344,28 +344,37 @@
     def rows_of(n):
         return pl.ds(pl.multiple_of(n * 64, 64), 64)
 
-    def scatter_x(src, n):
-        return [
-            remote(src.at[rows_of(off(t, d))], xr.at[n - 2, d - 1], xss.at[n, d - 1], xrs.at[n, d - 1], at_x(d))
-            for d in order
-        ]
-
-    def collect_x(src, n, copies):
-        total = src[rows_of(t), :].astype(F32)
+    def piece(n, p):
+        return pl.ds(pl.multiple_of(n * 64 + p * 32, 32), 32)
+
+    def scatter_x(src, n, p, d):
+        return remote(
+            src.at[piece(off(t, d), p)], xr.at[n, d - 1, pl.ds(p * 32, 32)], xss.at[n * 2 + p, d - 1],
+            xrs.at[n * 2 + p, d - 1], at_x(d),
+        )
+
+    def collect_x(src, n, p, copies):
+        whole = src[piece(t, p), :].astype(F32)
         for cp in copies:
             cp.wait_recv()
         for d in range(3):
-            total = total + xr[n - 2, d].astype(F32)
-        return total
-
-    def spread_x(buf, n):
-        return [
-            remote(buf.at[rows_of(t)], buf.at[rows_of(t)], xss.at[n, d - 1], xrs.at[n, d - 1], at_x(d))
-            for d in order
-        ]
-
-    ppb[...] = pp[...].astype(BF)
-    post_c = scatter_x(ppb, 2)
+            whole = whole + xr[n, d, p * 32 : p * 32 + 32, :].astype(F32)
+        return whole
+
+    def spread_x(buf, n, p):
+        ref = buf.at[piece(t, p)]
+        return [remote(ref, ref, yss.at[n * 2 + p, d - 1], yrs.at[n * 2 + p, d - 1], at_x(d)) for d in order]
+
+    post_c = [[], []]
+    for pair in ((2, 1), (3, 0)):
+        lhs = [jnp.concatenate([ref[rows_of(off(t, d)), :] for d in pair], 0) for ref in (gg, ug)]
+        part = (dot(lhs[0], wg[...], NT) + dot(lhs[1], wu[...], NT)).astype(BF)
+        for n, d in enumerate(pair):
+            ppb[rows_of(off(t, d)), :] = part[n * 64 : n * 64 + 64]
+        for p in range(2):
+            for d in pair:
+                if d > 0:
+                    post_c[p].append(scatter_x(ppb, 0, p, d))
     mpb[...] = dot(hid[...], wd[...]).astype(BF)
 
     def core_stage(g, r, ss, qs, y):
@@ -430,12 +439,15 @@
         weight_part(g1, post, ug, FF, y)
         core1.append(core_stage(g1, r1, s1, q1, y))
 
-    post_grad = collect_x(ppb, 2, post_c)
-    back, post_gain_term = row_norm_back(mid[rows_of(t), :], pg[...], post_grad)
-    mgr[...] = gy[rows_of(t), :].astype(F32) + back
-    ml[rows_of(t), :] = mgr[...].astype(BF)
-    ml_c = spread_x(ml, 4)
-    gv[0, 1:2, :] = jnp.sum(post_gain_term, 0, keepdims=True)
+    ml_c = []
+    for p in range(2):
+        post_grad = collect_x(ppb, 0, p, post_c[p])
+        back, term = row_norm_back(mid[piece(t, p), :], pg[...], post_grad)
+        mgr[p * 32 : p * 32 + 32, :] = gy[piece(t, p), :].astype(F32) + back
+        ml[piece(t, p), :] = mgr[p * 32 : p * 32 + 32, :].astype(BF)
+        ml_c += spread_x(ml, 0, p)
+        gain = jnp.sum(term, 0, keepdims=True)
+        post_gain_term = gain if p == 0 else post_gain_term + gain
 
     for y in range(4):
         core_sum(g1, r1, y, core1[y])
@@ -445,7 +457,7 @@
         weight_part(g3, gy, hid, 0, y)
     for cp in ml_c:
         cp.wait_recv()
-    mlp_c = scatter_x(mpb, 3)
+    mlp_c = [[scatter_x(mpb, 1, p, d) for d in order] for p in range(2)]
 
     ag = dot(ml[...], wo_all[t], NT).astype(BF).astype(F32)
     for kv in range(2):
@@ -544,8 +556,10 @@
         dql[:, kv * 128 : (kv + 1) * 128] = back.astype(BF)
         query_gain_term = query_gain_term + jnp.sum(term, 0, keepdims=True)
 
-    mixed_s[rows_of(t), :] = (mid[rows_of(t), :] + collect_x(mpb, 3, mlp_c)).astype(BF)
-    mixed_c = spread_x(mixed_s, 5)
+    mixed_c = []
+    for p in range(2):
+        mixed_s[piece(t, p), :] = (mid[piece(t, p), :] + collect_x(mpb, 1, p, mlp_c[p])).astype(BF)
+        mixed_c += spread_x(mixed_s, 1, p)
 
     first_sum(r0, ra0, first0)
     second0 = second_stage(r0, rb0, s0, q0)
@@ -566,10 +580,7 @@
     key_gain_term = jnp.sum(term, 0, keepdims=True)
 
     ipb[...] = (pp[...] + dot(kvl[:, 0:128], wk[...], NT) + dot(kvl[:, 128:256], wv[...], NT)).astype(BF)
-    in_c = [
-        remote(ipb.at[rows_of(off(t, d))], xr.at[2, d - 1], xss.at[6, d - 1], xrs.at[6, d - 1], at_x(d))
-        for d in order
-    ]
+    in_c = [[scatter_x(ipb, 2, p, d) for d in order] for p in range(2)]
     for y in range(4):
         core_sum(g3, r3, y, core3[y])
     first3 = first_stage(r3, ra3, s3, q3)
@@ -585,18 +596,7 @@
         core_sum(g2, r2, y, core2[y])
     first2 = first_stage(r2, ra2, s2, q2)
 
-    total = ipb[rows_of(t), :].astype(F32)
-    for cp in in_c:
-        cp.wait_recv()
-    for d in range(3):
-        total = total + xr[2, d].astype(F32)
-    back, term = row_norm_back(x[rows_of(t), :].astype(F32), ng[...], total)
-    gv[0, 0:1, :] = jnp.sum(term, 0, keepdims=True)
-    gv[0, 2:8, :] = jnp.zeros((6, 1024), F32)
-    gv[0, 2:3, 0:128] = query_gain_term + pltpu.roll(query_gain_term, 64, 1)
-    gv[0, 3:4, 0:128] = key_gain_term + pltpu.roll(key_gain_term, 64, 1)
-
-    bases = (0, 3, 4, 7)
+    bases = (0, 3, 10)
 
     def gain_stage(n, peers):
         return [
@@ -605,31 +605,40 @@
         ]
 
     def gain_sum(n, copies):
-        total = gv[n]
+        whole = gv[n]
         for i, cp in enumerate(copies):
             cp.wait_recv()
-            total = total + gr[bases[n] + i]
-        return total
-
-    gain_c = gain_stage(0, [at_x(d) for d in order])
-    xg_s[rows_of(t), :] = (mgr[...] + back).astype(BF)
-    xg_c = [
-        remote(xg_s.at[rows_of(t)], xg_s.at[rows_of(t)], xss.at[7, d - 1], xrs.at[7, d - 1], at_x(d))
-        for d in order
-    ]
+            whole = whole + gr[bases[n] + i]
+        return whole
+
+    gv[0, 1:2, :] = post_gain_term
+    gv[0, 2:8, :] = jnp.zeros((6, 1024), F32)
+    gv[0, 2:3, 0:128] = query_gain_term + pltpu.roll(query_gain_term, 64, 1)
+    gv[0, 3:4, 0:128] = key_gain_term + pltpu.roll(key_gain_term, 64, 1)
+    xg_c = []
+    for p in range(2):
+        back, term = row_norm_back(
+            x[piece(t, p), :].astype(F32), ng[...], collect_x(ipb, 2, p, in_c[p])
+        )
+        gain = jnp.sum(term, 0, keepdims=True)
+        xg_s[piece(t, p), :] = (mgr[p * 32 : p * 32 + 32, :] + back).astype(BF)
+        if p == 0:
+            norm_gain_term = gain
+        else:
+            gv[0, 0:1, :] = norm_gain_term + gain
+            gain_c = gain_stage(0, [at_x(d) for d in order])
+        xg_c += spread_x(xg_s, 2, p)
     gv[1] = gain_sum(0, gain_c)
-    gain_c = gain_stage(1, [at_k])
+    gain_c = gain_stage(1, [at_k] + [at_y(d) for d in order] + [at_ky(d) for d in order])
+    first_sum(r2, ra2, first2)
+    second2 = second_stage(r2, rb2, s2, q2)
     first_sum(r3, ra3, first3)
     second3 = second_stage(r3, rb3, s3, q3)
     gv[2] = gain_sum(1, gain_c)
-    gain_c = gain_stage(2, [at_y(d) for d in order])
-    first_sum(r2, ra2, first2)
-    second2 = second_stage(r2, rb2, s2, q2)
+    gain_c = gain_stage(2, [at_z(d) for d in order])
     for cp in mixed_c:
         cp.wait_recv()
     mixed_out[...] = mixed_s[...]
-    gv[3] = gain_sum(2, gain_c)
-    gain_c = gain_stage(3, [at_z(d) for d in order])
     for half, total in enumerate(second_sum(r3, rb3, second3)):
         rows = slice(half * 16, half * 16 + 16)
         down_out[rows, :] = total[:, 0:FF]
@@ -639,10 +648,10 @@
         rows = slice(half * 16, half * 16 + 16)
         wk_out[rows, :] = total[:, 0:128]
         wv_out[rows, :] = total[:, 128:256]
+    gains = gain_sum(2, gain_c)
     for cp in xg_c:
         cp.wait_recv()
     xgrad_out[...] = xg_s[...]
-    gains = gain_sum(3, gain_c)
     ng_out[...] = gains[0:1, :]
     pg_out[...] = gains[1:2, :]
     qg_out[...] = gains[2:3, 0:64]
@@ -674,7 +683,8 @@
         return [V(lead + (rows, width), BF) for lead in ((4, 4, 2, 2), (4, 4, 2), (2, 3, 4), (2, 3))]
 
     scratch = [
-        V((1024, FF), BF), V((1024, FF), BF), V((FF, 1024), BF), V((4, 256, 1024), BF),
+        V((1024, FF), BF), V((1024, FF), BF), V((FF, 1024), BF),
+        V((1024, 256), BF), V((256, 1024), BF), V((4, 256, 1024), BF),
         V((256, 1024), BF), V((2, 32, 256, 128), BF), V((256, 128), F32), V((2, 256, 128), F32),
         V((256, 128), F32), V((256, 128), F32), V((2, 512, 128), BF), V((2, 512, 128), BF),
         V((2, 2, 128, 256), F32), V((2, 2, 8, 256), F32), V((2, 8, 512), F32), V((4, 256, 256), BF),
@@ -687,9 +697,9 @@
         *ring(256, 128),
         *ring(16, G2X),
         *ring(16, G3X),
-        V((4, 8, 1024), F32), V((10, 8, 1024), F32),
-        sem(4), sem(2, 32), sem(2, 32), sem(9, 3), sem(9, 3), sem(3), sem(3),
-        *[sem(16)] * 8, sem(3, 4), sem(3, 4), sem(10), sem(10),
+        V((3, 8, 1024), F32), V((13, 8, 1024), F32),
+        sem(6), sem(2, 32), sem(2, 32), sem(9, 3), sem(9, 3), sem(6, 3), sem(6, 3), sem(3), sem(3),
+        *[sem(16)] * 8, sem(3, 4), sem(3, 4), sem(13), sem(13),
     ]
     shape = jax.ShapeDtypeStruct
     outs = [
@@ -702,7 +712,7 @@
         kernel,
         name="block",
         out_shape=outs,
-        in_specs=[vm] * 7 + [hbm] + [vm] + [hbm] * 3 + [vm] * 5,
+        in_specs=[vm] * 2 + [hbm] + [vm] * 4 + [hbm] + [vm] + [hbm] * 4 + [vm] * 4,
         out_specs=[vm] * 13,
         scratch_shapes=scratch,
         compiler_params=pltpu.CompilerParams(

time: 116 us -> 115 us (level); the launches traced: 116 us -> 114 us
  Pallas kernels: 115 us -> 113 us
    pallas_call x1, Pallas kernels: 113 us -> 110 us  [on_device(): pl.pallas_call(kernel, name='block', out_shape=outs, in_specs=[vm] * 2 +...]
where the time goes in v4:
time: 115 us; the launch traced here: 114 us
  Pallas kernels  113 us (98%)
    pallas_call x1, Pallas kernels, on_device(): pl.pallas_call(kernel, name='block', out_shape=outs, in_specs=[vm] * 2 +...  110 us
    pallas_call x1, Pallas kernels, on_device(): pl.pallas_call(hand_out, name='hand_out', out_shape=outs, in_specs=[vm] *...  2.58 us

profile of v4, /device:TPU:0, one launch (start us, length us, event | category | flops | bytes accessed | tf_op | source)
XLA Modules:
  0.0 113.8 jit_solution(337898262048244406)
XLA Ops:
  0.6 110.5 %block.1 = (bf16[256,1024]{1,0:T(8,128)(2,1)}, bf16[256,1024]{1,0:T(8,128)(2,1)}, f32[1,1024]{1,0:T(1,128)}, f32[32,256]{1,0:T(8,128)}, f32[32,128]{1,0:T(8,128)...) custom-call(bf16[256,1024]{1,0:T(8,128)(2,1)} %bitcast.18, ...), custom_call_target="tpu_custom_call" | custom-call | tf_op jit(solution)/shard_map/block/pallas_call | solution.py:711
  111.1 2.6 %hand_out.1 = (bf16[256,1024]{1,0:T(8,128)(2,1)}, bf16[256,1024]{1,0:T(8,128)(2,1)}, f32[1,1024]{1,0:T(1,128)}, f32[32,256]{1,0:T(8,128)}, f32[32,128]{1,0:T(8,1...) custom-call(bf16[256,1024]{1,0:T(8,128)(2,1)} %get-tuple-element.39., ...), custom_call_target="tpu_custom_call" | custom-call | tf_op jit(solution)/shard_map/hand_out/pallas_call | solution.py:726

commit v5 on v4

--- a/solution.py
+++ b/solution.py
@@ -384,7 +384,7 @@
         copy.wait_recv()
 
         def add(z, _):
-            r[y, z] = (g[y, z, ck].astype(F32) + r[y, z].astype(F32)).astype(BF)
+            r[y, z] = g[y, z, ck] + r[y, z]
             return 0
 
         lax.fori_loop(0, 4, add, 0)

time: 115 us -> 115 us (level)
  no operation moved by 1% of the time
where the time goes in v5:
time: 115 us; the launch traced here: 114 us
  Pallas kernels  113 us (98%)
    pallas_call x1, Pallas kernels, on_device(): pl.pallas_call(kernel, name='block', out_shape=outs, in_specs=[vm] * 2 +...  110 us
    pallas_call x1, Pallas kernels, on_device(): pl.pallas_call(hand_out, name='hand_out', out_shape=outs, in_specs=[vm] *...  2.58 us

profile of v5, /device:TPU:0, one launch (start us, length us, event | category | flops | bytes accessed | tf_op | source)
XLA Modules:
  0.0 113.7 jit_solution(5913866260578668965)
XLA Ops:
  0.6 110.3 %block.1 = (bf16[256,1024]{1,0:T(8,128)(2,1)}, bf16[256,1024]{1,0:T(8,128)(2,1)}, f32[1,1024]{1,0:T(1,128)}, f32[32,256]{1,0:T(8,128)}, f32[32,128]{1,0:T(8,128)...) custom-call(bf16[256,1024]{1,0:T(8,128)(2,1)} %bitcast.18, ...), custom_call_target="tpu_custom_call" | custom-call | tf_op jit(solution)/shard_map/block/pallas_call | solution.py:711
  111.0 2.6 %hand_out.1 = (bf16[256,1024]{1,0:T(8,128)(2,1)}, bf16[256,1024]{1,0:T(8,128)(2,1)}, f32[1,1024]{1,0:T(1,128)}, f32[32,256]{1,0:T(8,128)}, f32[32,128]{1,0:T(8,1...) custom-call(bf16[256,1024]{1,0:T(8,128)(2,1)} %get-tuple-element.39., ...), custom_call_target="tpu_custom_call" | custom-call | tf_op jit(solution)/shard_map/hand_out/pallas_call | solution.py:726
